TPU v7x, 32 devices: a whole 2x2x4 slice. The times are simulated.
32 devices in a mesh: grp: 2 (over y), space: 16 (over z, x, core).
Axes of the slice: x: 2, y: 2, z: 4, core: 2. Of those that a mesh axis runs over, the one named last changes fastest.
Arguments:
- gauge_links: bfloat16 [8, 2, 3, 3, 128, 2048], P('grp', None, None, None, None, 'space'), parts along dimension 0, may hold values from -2.5 to 2.5
- propagators: bfloat16 [4, 2, 4, 3, 128, 2048], P('grp', None, None, None, None, 'space'), parts along dimension 0, may hold values from -6 to 6
- sink_cotangent: bfloat16 [4, 2, 4, 3, 128, 2048], P('grp', None, None, None, 'space'), parts along dimension 0, may hold values from -6 to 6
- source_time: int32 [4], P('grp'), parts along dimension 0, may hold values from 0 to 7
- source_place: int32 [4, 3], P('grp'), parts along dimension 0, may hold values from 0 to 15
- pair_source: int32 [64], P('grp'), parts along dimension 0, may hold values from 0 to 1
- pair_separation: int32 [64], P('grp'), parts along dimension 0, may hold values from 0 to 7
- pair_owner: int32 [64, 1], P('grp'), parts along dimension 0, may hold values from 0 to 15; in each aligned block of 32 rows (0 to 31, 32 to 63, ...) at most 4 rows name the same one
Outputs:
- inserted: bfloat16 [4, 2, 4, 3, 128, 2048], P('grp', None, None, None, None, 'space'), parts along dimension 0
- correlator: float32 [128, 256], P(('grp', 'space')), parts along dimension 0
There are 2 independent parts, one for each index of `grp`. A program takes and returns all parts, laid end to end along the dimension named above; each array names one. Nothing has to cross between parts.
Inputs may be any that keep to these rules, and one draw needn't show every extreme that they name: `pair_owner`: at most 4 pairs share an owner, and some owner has exactly 4.
All inputs are finite; a program needn't handle non-finite values.
Results may differ from a plain program's by a relative error of at most 0.0032.
Values may be sent and summed in bfloat16 or wider, within the bound.
No kernel may reach another device: no remote copies, remote signals or barrier semaphores. Data moves between devices by JAX's collectives and lax.ppermute only.
A program may use at most 256 MiB of HBM per device.

v0:
```python
import functools
import math

import jax
import jax.numpy as jnp
import numpy as np
from jax import lax
from jax.experimental import pallas as pl
from jax.experimental.pallas import tpu as pltpu
from jax.sharding import PartitionSpec as P

LT = 8
LX = 16
LY = 128
TX = LT * LX
NMOM = 128
SLOTS = 4
OUTPUT_SCALE = 0.1
F32 = jnp.float32
BF16 = jnp.bfloat16
VMEM_BYTES = 56 * 1024 * 1024
UPPER = ((0, 1), (0, 2), (1, 2))
SYMMETRIC = ((0, 0), (1, 1), (2, 2), (0, 1), (0, 2), (1, 2))
HALF = len(UPPER) + len(SYMMETRIC)


def from_behind(block, distance):
    count = lax.axis_size("space")
    return lax.ppermute(block, "space", [((i - distance) % count, i) for i in range(count)])


def entry(left, right, row, col, left_dagger, right_dagger, part):
    total = None
    for inner in range(3):
        a_re, a_im = left[inner][row] if left_dagger else left[row][inner]
        b_re, b_im = right[col][inner] if right_dagger else right[inner][col]
        if part == 0:
            first, second = a_re * b_re, a_im * b_im
            negative = left_dagger == right_dagger
        elif left_dagger:
            first, second = a_re * b_im, a_im * b_re
            negative = True
        else:
            first, second = a_im * b_re, a_re * b_im
            negative = right_dagger
        total = first if total is None else total + first
        total = total - second if negative else total + second
    return total


def product(left, right, left_dagger=False, right_dagger=False):
    return [
        [
            tuple(entry(left, right, i, j, left_dagger, right_dagger, part) for part in (0, 1))
            for j in range(3)
        ]
        for i in range(3)
    ]


def anti_product(left, right):
    kept = []
    for i, j in UPPER:
        kept.append(entry(left, right, i, j, False, False, 0) - entry(left, right, j, i, False, False, 0))
    for i, j in SYMMETRIC:
        value = entry(left, right, i, j, False, False, 1)
        kept.append(value + (value if i == j else entry(left, right, j, i, False, False, 1)))
    return kept


def minus_adjoint(left, right):
    return [
        [
            (left[i][j][0] - right[j][i][0], left[i][j][1] + right[j][i][1])
            for j in range(3)
        ]
        for i in range(3)
    ]


def mapped(function, matrix):
    return [[tuple(function(part) for part in item) for item in row] for row in matrix]


def rows_of(time):
    return pl.ds(pl.multiple_of(time * LX, LX), LX)


def next_time(time):
    return lax.rem(time + 1, LT)


def last_time(time):
    return lax.rem(time + LT - 1, LT)


def load_matrix(ref, direction, time):
    rows = rows_of(time)
    return [
        [tuple(ref[direction, part, i, j, rows, :].astype(F32) for part in (0, 1)) for j in range(3)]
        for i in range(3)
    ]


def up_x(value):
    return pltpu.roll(value, LX - 1, 0)


def down_x(value):
    return pltpu.roll(value, 1, 0)


def up_y(value):
    return pltpu.roll(value, LY - 1, 1)


def down_y(value):
    return pltpu.roll(value, 1, 1)


def neighbour_link(ref, direction, step, time):
    if step == 3:
        return load_matrix(ref, direction, next_time(time))
    return mapped(up_x if step == 0 else up_y, load_matrix(ref, direction, time))


def staple_kernel(links, out):
    def body(time, carry):
        rows = rows_of(time)
        up_link = load_matrix(links, 2, time)
        for slot, direction in enumerate((0, 1, 3)):
            left = product(up_link, load_matrix(links, direction, time), left_dagger=True)
            staple = product(left, neighbour_link(links, 2, direction, time))
            for i in range(3):
                for j in range(3):
                    for part in (0, 1):
                        out[slot, part, i, j, rows, :] = staple[i][j][part].astype(BF16)
        return carry

    lax.fori_loop(0, LT, body, 0)


def flat_kernel(links, out, corner):
    def lower(time, carry):
        rows = rows_of(time)
        for slot, direction in enumerate((0, 1)):
            bent = product(
                load_matrix(links, direction, time), neighbour_link(links, 3, direction, time)
            )
            bent = product(load_matrix(links, 3, time), bent, left_dagger=True)
            for i in range(3):
                for j in range(3):
                    for part in (0, 1):
                        corner[slot, part, i, j, rows, :] = bent[i][j][part]
        return carry

    lax.fori_loop(0, LT, lower, 0)

    def upper(time, carry):
        rows = rows_of(time)
        for slot, direction in enumerate((0, 1)):
            far = product(
                load_matrix(links, 3, time), neighbour_link(links, direction, 3, time)
            )
            far = product(neighbour_link(links, 3, direction, time), far, right_dagger=True)
            bend = minus_adjoint(far, load_matrix(corner, slot, last_time(time)))
            link = load_matrix(links, direction, time)
            ahead = anti_product(link, bend)
            behind = anti_product(bend, link)
            move = down_x if direction == 0 else down_y
            for index in range(HALF):
                out[(slot + 1) * HALF + index, rows, :] = ahead[index] + move(behind[index])
        link_x, link_y = load_matrix(links, 0, time), load_matrix(links, 1, time)
        over_x, over_y = mapped(up_y, link_x), mapped(up_x, link_y)
        near = product(link_x, product(link_y, over_x), left_dagger=True)
        far = product(over_x, product(link_x, over_y), right_dagger=True)
        bend = minus_adjoint(far, mapped(down_x, near))
        ahead = anti_product(link_y, bend)
        behind = anti_product(bend, link_y)
        for index in range(HALF):
            out[index, rows, :] = -(ahead[index] + down_y(behind[index]))
        return carry

    lax.fori_loop(0, LT, upper, 0)


def insert_kernel(links, above, staples, flat, plain, inserted, crossed, rise, behind_t):
    def planes(time, carry):
        rows = rows_of(time)
        up_link = load_matrix(links, 2, time)
        for slot, direction in enumerate((0, 1, 3)):
            far = product(up_link, load_matrix(above, slot, time))
            far = product(neighbour_link(links, 2, direction, time), far, right_dagger=True)
            bend = minus_adjoint(far, load_matrix(staples, slot, time))
            link = load_matrix(links, direction, time)
            ahead = anti_product(link, bend)
            behind = anti_product(bend, link)
            for index in range(HALF):
                if direction == 3:
                    rise[slot * HALF + index, rows, :] = ahead[index]
                    behind_t[index, rows, :] = behind[index]
                else:
                    move = down_x if direction == 0 else down_y
                    rise[slot * HALF + index, rows, :] = ahead[index] + move(behind[index])
        return carry

    lax.fori_loop(0, LT, planes, 0)

    def insertion(time, carry):
        rows = rows_of(time)
        before = rows_of(last_time(time))
        for block in range(2):
            sign = 1.0 if block == 0 else -1.0

            def field(number):
                parts = []
                for index in range(HALF):
                    if number == 0:
                        value = sign * flat[HALF + index, rows, :] - rise[HALF + index, rows, :]
                    elif number == 1:
                        value = -sign * flat[2 * HALF + index, rows, :] - rise[index, rows, :]
                    else:
                        last = rise[2 * HALF + index, rows, :] + behind_t[index, before, :]
                        value = -flat[index, rows, :] - sign * last
                    parts.append(value * 0.125)
                trace = (parts[3] + parts[4] + parts[5]) * (1.0 / 3.0)
                for index in (3, 4, 5):
                    parts[index] = parts[index] - trace
                matrix = [[None] * 3 for _ in range(3)]
                for index, (i, j) in enumerate(UPPER):
                    re, im = parts[index], parts[6 + index]
                    matrix[i][j] = (re, im)
                    matrix[j][i] = (-re, im)
                for i in range(3):
                    matrix[i][i] = (None, parts[3 + i])
                return matrix

            first, second, third = field(0), field(1), field(2)
            same = [
                [(-third[i][j][1], None if i == j else third[i][j][0]) for j in range(3)]
                for i in range(3)
            ]
            cross = [
                [
                    (
                        -first[i][j][1] if i == j else second[i][j][0] - first[i][j][1],
                        second[i][j][1] if i == j else first[i][j][0] + second[i][j][1],
                    )
                    for j in range(3)
                ]
                for i in range(3)
            ]
            for source in range(plain.shape[0]):
                spinor = [
                    [
                        tuple(
                            plain[source, part, 2 * block + spin, color, rows, :].astype(F32)
                            for part in (0, 1)
                        )
                        for color in range(3)
                    ]
                    for spin in range(2)
                ]
                for spin in range(2):
                    result = []
                    for i in range(3):
                        total_re = total_im = None
                        for j in range(3):
                            m_re, m_im = same[i][j]
                            v_re, v_im = spinor[spin][j]
                            re, im = m_re * v_re, m_re * v_im
                            if m_im is not None:
                                re, im = re - m_im * v_im, im + m_im * v_re
                            if spin == 0:
                                total_re = re if total_re is None else total_re + re
                                total_im = im if total_im is None else total_im + im
                            else:
                                total_re = -re if total_re is None else total_re - re
                                total_im = -im if total_im is None else total_im - im
                        for j in range(3):
                            v_re, v_im = spinor[1 - spin][j]
                            if spin == 0:
                                m_re, m_im = cross[i][j]
                                total_re = total_re + m_re * v_re - m_im * v_im
                                total_im = total_im + m_re * v_im + m_im * v_re
                            else:
                                m_re, m_im = cross[j][i]
                                total_re = total_re + m_re * v_re + m_im * v_im
                                total_im = total_im + m_re * v_im - m_im * v_re
                        kept = (total_re.astype(BF16), total_im.astype(BF16))
                        for part in (0, 1):
                            inserted[source, part, 2 * block + spin, i, rows, :] = kept[part]
                        result.append(tuple(part.astype(F32) for part in kept))
                    for a, b, c in ((0, 1, 2), (1, 2, 0), (2, 0, 1)):
                        a_re, a_im = result[a]
                        b_re, b_im = result[b]
                        p_re, p_im = spinor[spin][a]
                        q_re, q_im = spinor[spin][b]
                        crossed[source, 0, 2 * block + spin, c, rows, :] = (
                            a_re * q_re - a_im * q_im - b_re * p_re + b_im * p_im
                        )
                        crossed[source, 1, 2 * block + spin, c, rows, :] = (
                            a_re * q_im + a_im * q_re - b_re * p_im - b_im * p_re
                        )
        return carry

    lax.fori_loop(0, LT, insertion, 0)


def project_kernel(sources, crossed, sink, wave_y, wave_x, turn, owner, out, density):
    count = sources * LT * LX

    def body(time, carry):
        rows = rows_of(time)
        for source in range(sources):
            total_re = total_im = None
            for spin in range(4):
                for color in range(3):
                    eta = []
                    for part in (0, 1):
                        line = (((source * 2 + part) * 4) + spin) * 3 + color
                        eta.append(
                            jnp.concatenate(
                                [sink[2 * time + half, pl.ds(line * 8, 8), :] for half in (0, 1)],
                                axis=0,
                            ).astype(F32)
                        )
                    w_re = crossed[source, 0, spin, color, rows, :]
                    w_im = crossed[source, 1, spin, color, rows, :]
                    re = w_re * eta[0] - w_im * eta[1]
                    im = w_re * eta[1] + w_im * eta[0]
                    total_re = re if total_re is None else total_re + re
                    total_im = im if total_im is None else total_im + im
            place = pl.multiple_of(source * TX + time * LX, LX)
            density[pl.ds(place, LX), :] = total_re
            density[pl.ds(pl.multiple_of(count + place, LX), LX), :] = total_im
        return carry

    lax.fori_loop(0, LT, body, 0)
    values = density[...]
    high = values.astype(BF16)
    low = (values - high.astype(F32)).astype(BF16)
    both = functools.partial(jnp.dot, preferred_element_type=F32)
    waves = both(high, wave_y[0]) + (both(low, wave_y[0]) + both(high, wave_y[1]))
    cos_re, sin_re = waves[:count, :NMOM], waves[:count, NMOM:]
    cos_im, sin_im = waves[count:, :NMOM], waves[count:, NMOM:]
    line_re = (cos_re + sin_im).reshape(sources * LT, LX, NMOM)
    line_im = (cos_im - sin_re).reshape(sources * LT, LX, NMOM)
    cos_x, sin_x = wave_x[0][None], wave_x[1][None]
    sum_re = jnp.sum(line_re * cos_x + line_im * sin_x, axis=1)
    sum_im = jnp.sum(line_im * cos_x - line_re * sin_x, axis=1)
    cos_t, sin_t = turn[0], turn[1]
    turned = jnp.concatenate(
        [sum_re * cos_t - sum_im * sin_t, sum_re * sin_t + sum_im * cos_t], axis=1
    )
    out[...] = jnp.dot(
        owner[...], turned, precision=lax.Precision.HIGHEST, preferred_element_type=F32
    )


def spread_kernel(sink, out):
    for device in range(out.shape[0]):
        piece = sink[:, :, device * LY : (device + 1) * LY].astype(F32)
        out[device] = piece.reshape(out.shape[1], LY).astype(BF16)


def params():
    return pltpu.CompilerParams(vmem_limit_bytes=VMEM_BYTES)


def whole(count):
    return [pl.BlockSpec(memory_space=pltpu.VMEM)] * count


def cost(flops, moved):
    return pl.CostEstimate(flops=flops, bytes_accessed=moved, transcendentals=0)


def momenta():
    index = np.arange(NMOM)
    return index % 4 - 1, index // 4 % 4 - 1, index // 16 - NMOM // 32


def wave_tables():
    wave_x, wave_y, _ = momenta()
    angle_y = 2.0 * np.pi * ((wave_y[None, :] * np.arange(LY)[:, None]) % LY) / LY
    table = np.concatenate([np.cos(angle_y), np.sin(angle_y)], axis=1)
    high = table.astype(jnp.bfloat16)
    low = (table - high.astype(np.float64)).astype(jnp.bfloat16)
    angle_x = 2.0 * np.pi * ((wave_x[None, :] * np.arange(LX)[:, None]) % LX) / LX
    along_x = np.stack([np.cos(angle_x), np.sin(angle_x)]).astype(np.float32)
    return np.stack([high, low]), along_x


def turn_table(source_place, z_position, extent_z):
    wave_x, wave_y, wave_z = (jnp.asarray(w, jnp.int32)[None, :] for w in momenta())
    fraction = (
        (wave_x * source_place[:, 0:1] % LX).astype(F32) / LX
        + (wave_y * source_place[:, 1:2] % LY).astype(F32) / LY
        + (wave_z * (source_place[:, 2:3] - z_position) % extent_z).astype(F32) / extent_z
    )
    angle = 2.0 * math.pi * fraction
    scale = OUTPUT_SCALE / math.sqrt(LX * LY * extent_z)
    table = jnp.stack([jnp.cos(angle), jnp.sin(angle)]) * scale
    return jnp.repeat(table, LT, axis=1)


def owner_table(source_time, pair_source, pair_separation, pair_owner, row_count):
    sources = source_time.shape[0]
    pairs = pair_source.shape[0]
    hits = pair_source[:, None] == jnp.arange(sources, dtype=jnp.int32)[None, :]
    start = jnp.sum(jnp.where(hits, source_time[None, :], 0), axis=1)
    chosen = pair_source * LT + (start + pair_separation) % LT
    picks = chosen[:, None] == jnp.arange(sources * LT, dtype=jnp.int32)[None, :]
    owner = pair_owner[:, 0]
    number = jnp.arange(pairs, dtype=jnp.int32)
    earlier = (owner[:, None] == owner[None, :]) & (number[None, :] < number[:, None])
    target = owner * SLOTS + jnp.sum(earlier.astype(jnp.int32), axis=1)
    rows = jnp.arange(row_count, dtype=jnp.int32)[:, None] == target[None, :]
    return jnp.dot(rows.astype(BF16), picks.astype(BF16), preferred_element_type=F32)


def on_device(
    gauge_links,
    propagators,
    sink_cotangent,
    source_time,
    source_place,
    pair_source,
    pair_separation,
    pair_owner,
):
    devices = lax.axis_size("space")
    assert gauge_links.shape[5] == LY
    sources = propagators.shape[0]
    lines = sources * 2 * 4 * 3
    slab = TX // devices
    site = (TX, LY)

    above = jnp.concatenate(
        [from_behind(gauge_links[0:2], -1), from_behind(gauge_links[3:4], -1)], axis=0
    )
    own_staples = pl.pallas_call(
        staple_kernel,
        out_shape=jax.ShapeDtypeStruct((3, 2, 3, 3) + site, BF16),
        in_specs=whole(1),
        out_specs=whole(1)[0],
        compiler_params=params(),
        cost_estimate=cost(6 * 216 * TX * LY, 4 << 20),
        name="staples",
    )(gauge_links)
    staples = from_behind(own_staples, 1)

    if slab == 8:
        spread = pl.pallas_call(
            spread_kernel,
            out_shape=jax.ShapeDtypeStruct((devices, lines * slab, LY), BF16),
            in_specs=whole(1),
            out_specs=whole(1)[0],
            compiler_params=params(),
            cost_estimate=cost(lines * TX * LY, 3 << 20),
            name="spread",
        )(sink_cotangent.reshape(lines, slab, devices * LY))
    else:
        spread = (
            sink_cotangent.reshape(lines, slab, devices, LY)
            .transpose(2, 0, 1, 3)
            .reshape(devices, lines * slab, LY)
        )
    sink = lax.all_to_all(spread, "space", split_axis=0, concat_axis=0, tiled=True)
    if slab != 8:
        sink = (
            sink.reshape(TX // 8, 8 // slab, lines, slab, LY)
            .transpose(0, 2, 1, 3, 4)
            .reshape(TX // 8, lines * 8, LY)
        )

    flat = pl.pallas_call(
        flat_kernel,
        out_shape=jax.ShapeDtypeStruct((3 * HALF,) + site, F32),
        in_specs=whole(1),
        out_specs=whole(1)[0],
        scratch_shapes=[pltpu.VMEM((2, 2, 3, 3) + site, F32)],
        compiler_params=params(),
        cost_estimate=cost(18 * 200 * TX * LY, 4 << 20),
        name="flat_planes",
    )(gauge_links)

    inserted, crossed = pl.pallas_call(
        insert_kernel,
        out_shape=(
            jax.ShapeDtypeStruct(propagators.shape, BF16),
            jax.ShapeDtypeStruct(propagators.shape, F32),
        ),
        in_specs=whole(5),
        out_specs=tuple(whole(2)),
        scratch_shapes=[pltpu.VMEM((3 * HALF,) + site, F32), pltpu.VMEM((HALF,) + site, F32)],
        compiler_params=params(),
        cost_estimate=cost(5000 * TX * LY, 12 << 20),
        name="insertion",
    )(gauge_links, above, staples, flat, propagators)

    table_y, table_x = wave_tables()
    turn = turn_table(source_place, lax.axis_index("space"), devices)
    owner = owner_table(
        source_time, pair_source, pair_separation, pair_owner, devices * SLOTS
    )
    rows = pl.pallas_call(
        functools.partial(project_kernel, sources),
        out_shape=jax.ShapeDtypeStruct((devices * SLOTS, 2 * NMOM), F32),
        in_specs=whole(6),
        out_specs=whole(1)[0],
        scratch_shapes=[pltpu.VMEM((2 * sources * TX, LY), F32)],
        compiler_params=params(),
        cost_estimate=cost(300 * TX * LY, 5 << 20),
        name="projection",
    )(crossed, sink, jnp.asarray(table_y), jnp.asarray(table_x), turn, owner)
    parts = lax.all_to_all(
        rows.reshape(devices, SLOTS, 2 * NMOM), "space", split_axis=0, concat_axis=0, tiled=True
    )
    return inserted, jnp.sum(parts, axis=0)


def solution(mesh):
    placed = (
        P("grp", None, None, None, None, "space"),
        P("grp", None, None, None, None, "space"),
        P("grp", None, None, None, "space", None),
        P("grp"),
        P("grp", None),
        P("grp"),
        P("grp"),
        P("grp", None),
    )
    return jax.shard_map(
        on_device,
        mesh=mesh,
        in_specs=placed,
        out_specs=(P("grp", None, None, None, None, "space"), P(("grp", "space"), None)),
        check_vma=False,
    )
```

profile of v0, /device:TPU:0, one launch (start us, length us, event | category | flops | bytes accessed | tf_op | source)
XLA Modules:
  0.0 104.7 jit_solution(7266968576852568383)
XLA Ops:
  0.6 2.8 %spread.1 = bf16[16,384,128]{2,1,0:T(8,128)(2,1)} custom-call(bf16[48,8,2048]{2,1,0:T(8,128)(2,1)} %bitcast.5), custom_call_target="tpu_custom_call" | custom-call | flops 786432 | bytes 3145728 | tf_op jit(solution)/shard_map/spread/pallas_call | solution.py:455
  3.5 7.4 %all-to-all-start = ((bf16[16,384,128]{2,1,0:T(8,128)(2,1)}), bf16[16,384,128]{2,1,0:T(8,128)(2,1)}, u32[]{:S(2)}, u32[]{:S(2)}) async-start(bf16[16,384,128]{2,1,0:T(8,128)(2,1)} %spread.1), calls=%async_computation | async-start | bytes 3145728 | tf_op jit(solution)/shard_map/all_to_all | solution.py:470
  10.9 0.0 copy-start
  10.9 6.0 %staples.1 = bf16[3,2,3,3,128,128]{5,4,3,2,1,0:T(8,128)(2,1)} custom-call(bf16[4,2,3,3,128,128]{5,4,3,2,1,0:T(8,128)(2,1)} %links.5), custom_call_target="tpu_custom_call" | custom-call | flops 21233664 | bytes 4194304 | tf_op jit(solution)/shard_map/staples/pallas_call | solution.py:443
  16.8 0.0 copy-start.5
  16.8 0.0 copy-start.2
  16.8 0.0 copy-start.3
  16.8 0.0 copy-start.4
  16.9 0.4 collective-permute-start.2
  17.3 0.0 copy-done
  17.3 0.9 slice.16
  18.2 4.1 %collective-permute-start.1 = (bf16[1,2,3,3,128,128]{5,4,3,2,1,0:T(8,128)(2,1)}, bf16[1,2,3,3,128,128]{5,4,3,2,1,0:T(8,128)(2,1)S(1)}, u32[]{:S(2)}, u32[]{:S(2)}) collective-permute-start(bf16[1,2,3,3,128,128]{5,4,3,2,1,0:T(8,128)(2,1)} %slice.16), channel_id=1, source_target_pairs={{1,0},{2,1},{3,2},{4,3},{5,4},{6,5},{7,6},{8,7},{9,8},{10,9},{11,1... | collective-permute-start | bytes 1769480 | tf_op jit(solution)/shard_map/ppermute | solution.py:29
  22.2 1.1 %slice.15 = bf16[2,2,3,3,128,128]{5,4,3,2,1,0:T(8,128)(2,1)} slice(bf16[4,2,3,3,128,128]{5,4,3,2,1,0:T(8,128)(2,1)S(1)} %copy-done), slice={[0:2], [0:2], [0:3], [0:3], [0:128], [0:128]} | slice | bytes 2359296 | tf_op jit(solution)/shard_map/slice | solution.py:441
  23.4 0.4 collective-permute-start
  23.8 0.0 copy-done.5
  23.8 0.2 convert_reduce_fusion
  24.0 0.0 copy-done.2
  24.0 0.2 slice_reduce_fusion.1
  24.2 0.0 copy-done.3
  24.2 0.7 fusion.16
  24.9 0.8 fusion.20
  25.7 0.0 copy-done.4
  25.7 12.0 %flat_planes.1.flat = f32[27,128,128]{2,1,0:T(8,128)} custom-call(bf16[4,2,3,3,128,128]{5,4,3,2,1,0:T(8,128)(2,1)} %links.5), custom_call_target="tpu_custom_call" | custom-call | flops 58982400 | bytes 4194304 | tf_op jit(solution)/shard_map/flat_planes/pallas_call | solution.py:478
  37.8 0.6 broadcast_bitcast_fusion.turn
  38.4 0.8 fusion.owner
  39.2 4.6 %collective-permute-done.1 = bf16[1,2,3,3,128,128]{5,4,3,2,1,0:T(8,128)(2,1)S(1)} collective-permute-done((bf16[1,2,3,3,128,128]{5,4,3,2,1,0:T(8,128)(2,1)}, bf16[1,2,3,3,128,128]{5,4,3,2,1,0:T(8,128)(2,1)S(1)}, u32[]{:S(2)}, u32[]{:S(2)}) %collective-permute-start.1) | collective-permute-done | bytes 589856 | tf_op jit(solution)/shard_map/ppermute | solution.py:29
  43.8 12.6 %collective-permute-done = bf16[2,2,3,3,128,128]{5,4,3,2,1,0:T(8,128)(2,1)S(1)} collective-permute-done((bf16[2,2,3,3,128,128]{5,4,3,2,1,0:T(8,128)(2,1)}, bf16[2,2,3,3,128,128]{5,4,3,2,1,0:T(8,128)(2,1)S(1)}, u32[]{:S(2)}, u32[]{:S(2)}) %collective-permute-start) | collective-permute-done | bytes 1179680 | tf_op jit(solution)/shard_map/ppermute | solution.py:29
  56.5 1.4 %pad_maximum_fusion.above = bf16[3,2,3,3,128,128]{5,4,3,2,1,0:T(8,128)(2,1)} fusion(bf16[1,2,3,3,128,128]{5,4,3,2,1,0:T(8,128)(2,1)S(1)} %collective-permute-done.1, bf16[2,2,3,3,128,128]{5,4,3,2,1,0:T(8,128)(2,1)S(1)} %collective-permute-done), kind=kLoop, calls=%fused_computation | loop fusion | flops 884736 | bytes 3538944 | tf_op jit(solution)/shard_map/concatenate | solution.py:440
  57.8 3.6 %collective-permute-done.2.staples = bf16[3,2,3,3,128,128]{5,4,3,2,1,0:T(8,128)(2,1)S(1)} collective-permute-done((bf16[3,2,3,3,128,128]{5,4,3,2,1,0:T(8,128)(2,1)}, bf16[3,2,3,3,128,128]{5,4,3,2,1,0:T(8,128)(2,1)S(1)}, u32[]{:S(2)}, u32[]{:S(2)}) %collective-permute-start.2) | collective-permute-done | bytes 1769504 | tf_op jit(solution)/shard_map/ppermute | solution.py:29
  61.4 0.0 copy-start.1
  61.4 1.2 %copy-done.1 = bf16[3,2,3,3,128,128]{5,4,3,2,1,0:T(8,128)(2,1)} copy-done((bf16[3,2,3,3,128,128]{5,4,3,2,1,0:T(8,128)(2,1)}, bf16[3,2,3,3,128,128]{5,4,3,2,1,0:T(8,128)(2,1)S(1)}, u32[]{:S(2)}) %copy-start.1) | copy-done | bytes 1769496
  62.6 15.6 %insertion.1 = (bf16[2,2,4,3,128,128]{5,4,3,2,1,0:T(8,128)(2,1)}, f32[2,2,4,3,128,128]{5,4,3,2,1,0:T(8,128)}) custom-call(bf16[4,2,3,3,128,128]{5,4,3,2,1,0:T(8,128)(2,1)} %links.5, bf16[3,2,3,3,128,128]{5,4,3,2,1,0:T(8,128)(2,1)} %pad_maximum_fusion.above, bf16[3,2,3,3,128,128]{5,4,3,2,1,0:T(8,128)(2,1)} %copy-done.1, f32[27,128,128]{2,1,0:T(8,128)} %flat_planes.1.flat, ...), custom_call_target="tpu_custom_call" | custom-call | flops 81920000 | bytes 12582912 | tf_op jit(solution)/shard_map/insertion/pallas_call | solution.py:489
  78.3 0.0 all-to-all-done.sink
  78.3 4.4 %projection.1 = f32[64,256]{1,0:T(8,128)} custom-call(f32[2,2,4,3,128,128]{5,4,3,2,1,0:T(8,128)} %get-tuple-element.5.crossed, bf16[16,384,128]{2,1,0:T(8,128)(2,1)} %all-to-all-done.sink, bf16[2,128,256]{2,1,0:T(8,128)(2,1)} %constant.79.clone.wave_y, f32[2,16,128]{2,1,0:T(8,128)} %constant.80.clone.wave_x, f32[2,16,128]{2,1,0:T(8,128)} %broadcast_bitcast_fusion.turn, ...), custom_call_target="tpu_custom_call" | custom-call | flops 4915200 | bytes 5242880 | tf_op jit(solution)/shard_map/projection/pallas_call | solution.py:508
  82.7 0.9 reshape.462
  83.5 20.6 %all_to_all.10 = f32[16,4,256]{2,1,0:T(4,128)S(1)} all-to-all(f32[16,4,256]{2,1,0:T(4,128)S(1)} %reshape.462), channel_id=1, replica_groups=mesh['grp'=2,'space'=16] {'space'}, dimensions={0} | all-to-all | bytes 131072 | tf_op jit(solution)/shard_map/all_to_all | solution.py:518
  104.1 0.6 reduce_sum.29
  (2 shorter events, 0.0 us)
Async XLA Ops:
  3.5 74.8 %all-to-all-start = ((bf16[16,384,128]{2,1,0:T(8,128)(2,1)}), bf16[16,384,128]{2,1,0:T(8,128)(2,1)}, u32[]{:S(2)}, u32[]{:S(2)}) async-start(bf16[16,384,128]{2,1,0:T(8,128)(2,1)} %spread.1), calls=%async_computation | async-start | bytes 3145728 | tf_op jit(solution)/shard_map/all_to_all | solution.py:470
  10.9 6.4 %copy-start = (bf16[4,2,3,3,128,128]{5,4,3,2,1,0:T(8,128)(2,1)S(1)}, bf16[4,2,3,3,128,128]{5,4,3,2,1,0:T(8,128)(2,1)}, u32[]{:S(2)}) copy-start(bf16[4,2,3,3,128,128]{5,4,3,2,1,0:T(8,128)(2,1)} %links.5) | copy-start | bytes 7077892
  16.8 6.9 %copy-start.5 = (s32[32,1]{0,1:T(1,128)S(1)}, s32[32,1]{0,1:T(1,128)}, u32[]{:S(2)}) copy-start(s32[32,1]{0,1:T(1,128)} %param.20) | copy-start | bytes 388
  16.8 7.1 %copy-start.2 = (s32[2,3]{1,0:T(2,128)S(1)}, s32[2,3]{1,0:T(2,128)}, u32[]{:S(2)}) copy-start(s32[2,3]{1,0:T(2,128)} %param.17) | copy-start | bytes 76
  16.8 7.3 %copy-start.3 = (s32[32]{0:T(128)S(1)}, s32[32]{0:T(128)}, u32[]{:S(2)}) copy-start(s32[32]{0:T(128)} %param.18) | copy-start | bytes 388
  16.8 8.9 %copy-start.4 = (s32[32]{0:T(128)S(1)}, s32[32]{0:T(128)}, u32[]{:S(2)}) copy-start(s32[32]{0:T(128)} %param.19) | copy-start | bytes 388
  16.9 44.6 %collective-permute-start.2 = (bf16[3,2,3,3,128,128]{5,4,3,2,1,0:T(8,128)(2,1)}, bf16[3,2,3,3,128,128]{5,4,3,2,1,0:T(8,128)(2,1)S(1)}, u32[]{:S(2)}, u32[]{:S(2)}) collective-permute-start(bf16[3,2,3,3,128,128]{5,4,3,2,1,0:T(8,128)(2,1)} %staples.1), channel_id=1, source_target_pairs={{15,0},{0,1},{1,2},{2,3},{3,4},{4,5},{5,6},{6,7},{7,8},{8,9},{9,10... | collective-permute-start | bytes 5308424 | tf_op jit(solution)/shard_map/ppermute | solution.py:29
  18.2 25.7 %collective-permute-start.1 = (bf16[1,2,3,3,128,128]{5,4,3,2,1,0:T(8,128)(2,1)}, bf16[1,2,3,3,128,128]{5,4,3,2,1,0:T(8,128)(2,1)S(1)}, u32[]{:S(2)}, u32[]{:S(2)}) collective-permute-start(bf16[1,2,3,3,128,128]{5,4,3,2,1,0:T(8,128)(2,1)} %slice.16), channel_id=1, source_target_pairs={{1,0},{2,1},{3,2},{4,3},{5,4},{6,5},{7,6},{8,7},{9,8},{10,9},{11,1... | collective-permute-start | bytes 1769480 | tf_op jit(solution)/shard_map/ppermute | solution.py:29
  23.4 33.1 %collective-permute-start = (bf16[2,2,3,3,128,128]{5,4,3,2,1,0:T(8,128)(2,1)}, bf16[2,2,3,3,128,128]{5,4,3,2,1,0:T(8,128)(2,1)S(1)}, u32[]{:S(2)}, u32[]{:S(2)}) collective-permute-start(bf16[2,2,3,3,128,128]{5,4,3,2,1,0:T(8,128)(2,1)} %slice.15), channel_id=1, source_target_pairs={{1,0},{2,1},{3,2},{4,3},{5,4},{6,5},{7,6},{8,7},{9,8},{10,9},{11,1... | collective-permute-start | bytes 3538952 | tf_op jit(solution)/shard_map/ppermute | solution.py:29
  61.4 1.2 %copy-start.1 = (bf16[3,2,3,3,128,128]{5,4,3,2,1,0:T(8,128)(2,1)}, bf16[3,2,3,3,128,128]{5,4,3,2,1,0:T(8,128)(2,1)S(1)}, u32[]{:S(2)}) copy-start(bf16[3,2,3,3,128,128]{5,4,3,2,1,0:T(8,128)(2,1)S(1)} %collective-permute-done.2.staples) | copy-start | bytes 5308420
where the time goes:
time: 105 us
  Pallas kernels  40.8 us (39%)
  waiting for transfers between devices  20.8 us (20%)
  blocking collectives  20.6 us (20%)
  starting transfers between devices  12.3 us (12%)
  local copies, waits for them, and re-layouts  4.72 us (4%)
  other arithmetic  3.95 us (4%)
    ppermute x3, waiting for transfers between devices, from_behind(): lax.ppermute(block, 'space', [((i - distance) % count, i) for i in range(...  20.8 us
    all_to_all x1, blocking collectives, on_device(): lax.all_to_all(rows.reshape(devices, SLOTS, 2 * NMOM), 'space', split_axi...  20.6 us
    pallas_call x1, Pallas kernels, on_device(): pl.pallas_call(insert_kernel, out_shape=(jax.ShapeDtypeStruct(propagators...  15.6 us
    pallas_call x1, Pallas kernels, on_device(): pl.pallas_call(flat_kernel, out_shape=jax.ShapeDtypeStruct((3 * HALF,) +...  12 us
    all_to_all x1, starting transfers between devices, on_device(): lax.all_to_all(spread, 'space', split_axis=0, concat_axis=0, tiled=True)  7.4 us
    pallas_call x1, Pallas kernels, on_device(): pl.pallas_call(staple_kernel, out_shape=jax.ShapeDtypeStruct((3, 2, 3, 3)...  5.96 us
    ppermute x3, starting transfers between devices, from_behind(): lax.ppermute(block, 'space', [((i - distance) % count, i) for i in range(...  4.9 us
    pallas_call x1, Pallas kernels, on_device(): pl.pallas_call(functools.partial(project_kernel, sources), out_shape=jax....  4.39 us
  transfers between devices with their start and end apart: 4, of which 3 were waited for; matrix products, arithmetic and copies ran while one was open for 6% of the time, Pallas kernels for 32%

commit v1 on v0

--- a/solution.py
+++ b/solution.py
@@ -18,9 +18,11 @@
 OUTPUT_SCALE = 0.1
 F32 = jnp.float32
 BF16 = jnp.bfloat16
-VMEM_BYTES = 56 * 1024 * 1024
+PIECES = ((0, 4), (4, 8))
+PADDED = 8
 UPPER = ((0, 1), (0, 2), (1, 2))
 SYMMETRIC = ((0, 0), (1, 1), (2, 2), (0, 1), (0, 2), (1, 2))
+HALVES = (slice(0, 8), slice(8, 16))
 HALF = len(UPPER) + len(SYMMETRIC)
 
 
@@ -94,12 +96,18 @@
     return lax.rem(time + LT - 1, LT)
 
 
-def load_matrix(ref, direction, time):
-    rows = rows_of(time)
-    return [
-        [tuple(ref[direction, part, i, j, rows, :].astype(F32) for part in (0, 1)) for j in range(3)]
-        for i in range(3)
-    ]
+def load_matrix(ref, direction, time, half=None):
+    rows = rows_of(time) if not isinstance(time, int) else slice(time * LX, (time + 1) * LX)
+
+    def load(part, i, j):
+        value = ref[direction, part, i, j, rows, :].astype(F32)
+        return value if half is None else value[half]
+
+    return [[tuple(load(part, i, j) for part in (0, 1)) for j in range(3)] for i in range(3)]
+
+
+def halved(matrix, half):
+    return mapped(lambda value: value[half], matrix)
 
 
 def up_x(value):
@@ -124,9 +132,10 @@
     return mapped(up_x if step == 0 else up_y, load_matrix(ref, direction, time))
 
 
-def staple_kernel(links, out):
-    def body(time, carry):
-        rows = rows_of(time)
+def staple_kernel(links, *outs):
+    def body(out, begin, step, carry):
+        time = begin + step
+        rows = rows_of(step)
         up_link = load_matrix(links, 2, time)
         for slot, direction in enumerate((0, 1, 3)):
             left = product(up_link, load_matrix(links, direction, time), left_dagger=True)
@@ -137,7 +146,8 @@
                         out[slot, part, i, j, rows, :] = staple[i][j][part].astype(BF16)
         return carry
 
-    lax.fori_loop(0, LT, body, 0)
+    for out, (begin, end) in zip(outs, PIECES):
+        lax.fori_loop(0, end - begin, functools.partial(body, out, jnp.int32(begin)), 0)
 
 
 def flat_kernel(links, out, corner):
@@ -184,77 +194,81 @@
     lax.fori_loop(0, LT, upper, 0)
 
 
-def insert_kernel(links, above, staples, flat, plain, inserted, crossed, rise, behind_t):
-    def planes(time, carry):
-        rows = rows_of(time)
-        up_link = load_matrix(links, 2, time)
+def neighbour_up(links, later, step):
+    if step == 3:
+        return load_matrix(later, 0, 0)
+    return mapped(up_x if step == 0 else up_y, load_matrix(links, 2, 0))
+
+
+def z_planes(links, later, above, staples, rise, edge):
+    for half in HALVES:
+        up_link = load_matrix(links, 2, 0, half)
         for slot, direction in enumerate((0, 1, 3)):
-            far = product(up_link, load_matrix(above, slot, time))
-            far = product(neighbour_link(links, 2, direction, time), far, right_dagger=True)
-            bend = minus_adjoint(far, load_matrix(staples, slot, time))
-            link = load_matrix(links, direction, time)
-            ahead = anti_product(link, bend)
-            behind = anti_product(bend, link)
+            far = product(up_link, load_matrix(above, slot, 0, half))
+            moved = halved(neighbour_up(links, later, direction), half)
+            far = product(moved, far, right_dagger=True)
+            bend = minus_adjoint(far, load_matrix(staples, slot, 0, half))
+            link = load_matrix(links, direction, 0, half)
+            for index, value in enumerate(anti_product(link, bend)):
+                rise[slot * HALF + index, half, :] = value
+            for index, value in enumerate(anti_product(bend, link)):
+                if direction == 1:
+                    rise[HALF + index, half, :] += down_y(value)
+                else:
+                    edge[(0 if direction == 3 else HALF) + index, half, :] = value
+    for index in range(HALF):
+        rise[index] += down_x(edge[HALF + index])
+
+
+def coefficients(flat, rise, before, coef):
+    for block in range(2):
+        sign = 1.0 if block == 0 else -1.0
+
+        def field(number):
+            parts = []
             for index in range(HALF):
-                if direction == 3:
-                    rise[slot * HALF + index, rows, :] = ahead[index]
-                    behind_t[index, rows, :] = behind[index]
+                if number == 0:
+                    value = sign * flat[HALF + index] - rise[HALF + index]
+                elif number == 1:
+                    value = -sign * flat[2 * HALF + index] - rise[index]
                 else:
-                    move = down_x if direction == 0 else down_y
-                    rise[slot * HALF + index, rows, :] = ahead[index] + move(behind[index])
-        return carry
-
-    lax.fori_loop(0, LT, planes, 0)
-
-    def insertion(time, carry):
-        rows = rows_of(time)
-        before = rows_of(last_time(time))
-        for block in range(2):
-            sign = 1.0 if block == 0 else -1.0
-
-            def field(number):
-                parts = []
-                for index in range(HALF):
-                    if number == 0:
-                        value = sign * flat[HALF + index, rows, :] - rise[HALF + index, rows, :]
-                    elif number == 1:
-                        value = -sign * flat[2 * HALF + index, rows, :] - rise[index, rows, :]
+                    value = -flat[index] - sign * (rise[2 * HALF + index] + before[index])
+                parts.append(value * 0.125)
+            trace = (parts[3] + parts[4] + parts[5]) * (1.0 / 3.0)
+            for index in (3, 4, 5):
+                parts[index] = parts[index] - trace
+            return parts
+
+        first, second, third = field(0), field(1), field(2)
+        for index in range(HALF):
+            coef[block, index] = third[index] if index < 3 else -third[index]
+        place = HALF
+        for i in range(3):
+            for j in range(3):
+                if i == j:
+                    re, im = -first[3 + i], second[3 + i]
+                else:
+                    index = UPPER.index((min(i, j), max(i, j)))
+                    if i < j:
+                        re = second[index] - first[6 + index]
+                        im = first[index] + second[6 + index]
                     else:
-                        last = rise[2 * HALF + index, rows, :] + behind_t[index, before, :]
-                        value = -flat[index, rows, :] - sign * last
-                    parts.append(value * 0.125)
-                trace = (parts[3] + parts[4] + parts[5]) * (1.0 / 3.0)
-                for index in (3, 4, 5):
-                    parts[index] = parts[index] - trace
-                matrix = [[None] * 3 for _ in range(3)]
-                for index, (i, j) in enumerate(UPPER):
-                    re, im = parts[index], parts[6 + index]
-                    matrix[i][j] = (re, im)
-                    matrix[j][i] = (-re, im)
-                for i in range(3):
-                    matrix[i][i] = (None, parts[3 + i])
-                return matrix
-
-            first, second, third = field(0), field(1), field(2)
-            same = [
-                [(-third[i][j][1], None if i == j else third[i][j][0]) for j in range(3)]
-                for i in range(3)
-            ]
-            cross = [
-                [
-                    (
-                        -first[i][j][1] if i == j else second[i][j][0] - first[i][j][1],
-                        second[i][j][1] if i == j else first[i][j][0] + second[i][j][1],
-                    )
-                    for j in range(3)
-                ]
-                for i in range(3)
-            ]
-            for source in range(plain.shape[0]):
+                        re = -second[index] - first[6 + index]
+                        im = second[6 + index] - first[index]
+                coef[block, place] = re
+                coef[block, place + 1] = im
+                place += 2
+
+
+def insert_slice(coef, plain, inserted, crossed):
+    for block in range(2):
+        for source in range(plain.shape[0]):
+            rounded = {}
+            for half in HALVES:
                 spinor = [
                     [
                         tuple(
-                            plain[source, part, 2 * block + spin, color, rows, :].astype(F32)
+                            plain[source, part, 2 * block + spin, color].astype(F32)[half]
                             for part in (0, 1)
                         )
                         for color in range(3)
@@ -262,56 +276,133 @@
                     for spin in range(2)
                 ]
                 for spin in range(2):
-                    result = []
                     for i in range(3):
                         total_re = total_im = None
                         for j in range(3):
-                            m_re, m_im = same[i][j]
+                            v_re, v_im = spinor[1 - spin][j]
+                            row, column = (i, j) if spin == 0 else (j, i)
+                            place = HALF + 2 * (3 * row + column)
+                            m_re, m_im = coef[block, place, half, :], coef[block, place + 1, half, :]
+                            re, im = m_re * v_re, m_re * v_im
+                            total_re = re if total_re is None else total_re + re
+                            total_im = im if total_im is None else total_im + im
+                            if spin == 0:
+                                total_re = total_re - m_im * v_im
+                                total_im = total_im + m_im * v_re
+                            else:
+                                total_re = total_re + m_im * v_im
+                                total_im = total_im - m_im * v_re
+                        for j in range(3):
                             v_re, v_im = spinor[spin][j]
-                            re, im = m_re * v_re, m_re * v_im
+                            if i == j:
+                                m_re, m_im = coef[block, 3 + i, half, :], None
+                            else:
+                                index = UPPER.index((min(i, j), max(i, j)))
+                                m_re = coef[block, 6 + index, half, :]
+                                m_im = coef[block, index, half, :]
+                            if spin == 0:
+                                total_re = total_re + m_re * v_re
+                                total_im = total_im + m_re * v_im
+                            else:
+                                total_re = total_re - m_re * v_re
+                                total_im = total_im - m_re * v_im
                             if m_im is not None:
-                                re, im = re - m_im * v_im, im + m_im * v_re
-                            if spin == 0:
-                                total_re = re if total_re is None else total_re + re
-                                total_im = im if total_im is None else total_im + im
-                            else:
-                                total_re = -re if total_re is None else total_re - re
-                                total_im = -im if total_im is None else total_im - im
-                        for j in range(3):
-                            v_re, v_im = spinor[1 - spin][j]
-                            if spin == 0:
-                                m_re, m_im = cross[i][j]
-                                total_re = total_re + m_re * v_re - m_im * v_im
-                                total_im = total_im + m_re * v_im + m_im * v_re
-                            else:
-                                m_re, m_im = cross[j][i]
-                                total_re = total_re + m_re * v_re + m_im * v_im
-                                total_im = total_im + m_re * v_im - m_im * v_re
-                        kept = (total_re.astype(BF16), total_im.astype(BF16))
-                        for part in (0, 1):
-                            inserted[source, part, 2 * block + spin, i, rows, :] = kept[part]
-                        result.append(tuple(part.astype(F32) for part in kept))
-                    for a, b, c in ((0, 1, 2), (1, 2, 0), (2, 0, 1)):
-                        a_re, a_im = result[a]
-                        b_re, b_im = result[b]
-                        p_re, p_im = spinor[spin][a]
-                        q_re, q_im = spinor[spin][b]
-                        crossed[source, 0, 2 * block + spin, c, rows, :] = (
-                            a_re * q_re - a_im * q_im - b_re * p_re + b_im * p_im
-                        )
-                        crossed[source, 1, 2 * block + spin, c, rows, :] = (
-                            a_re * q_im + a_im * q_re - b_re * p_im - b_im * p_re
-                        )
-        return carry
-
-    lax.fori_loop(0, LT, insertion, 0)
+                                if (i < j) == (spin == 0):
+                                    total_re = total_re - m_im * v_im
+                                    total_im = total_im + m_im * v_re
+                                else:
+                                    total_re = total_re + m_im * v_im
+                                    total_im = total_im - m_im * v_re
+                        for part, total in enumerate((total_re, total_im)):
+                            rounded.setdefault((spin, i, part), []).append(total)
+            for spin in range(2):
+                result = []
+                for i in range(3):
+                    kept = []
+                    for part in (0, 1):
+                        value = jnp.concatenate(rounded[spin, i, part], axis=0).astype(BF16)
+                        inserted[source, part, 2 * block + spin, i] = value
+                        kept.append(value.astype(F32))
+                    result.append(kept)
+                vector = [
+                    [plain[source, part, 2 * block + spin, color].astype(F32) for part in (0, 1)]
+                    for color in range(3)
+                ]
+                for a, b, c in ((0, 1, 2), (1, 2, 0), (2, 0, 1)):
+                    (a_re, a_im), (b_re, b_im) = result[a], result[b]
+                    (p_re, p_im), (q_re, q_im) = vector[a], vector[b]
+                    crossed[source, 0, 2 * block + spin, c] = (
+                        a_re * q_re - a_im * q_im - b_re * p_re + b_im * p_im
+                    )
+                    crossed[source, 1, 2 * block + spin, c] = (
+                        a_re * q_im + a_im * q_re - b_re * p_im - b_im * p_re
+                    )
+
+
+def insert_kernel(begin, end, *refs):
+    first, last = begin == 0, end == LT
+    refs = list(refs)
+    links, later, above, staples, flat, plain = refs[:6]
+    refs = refs[6:]
+    if not first:
+        edge_in = refs.pop(0)
+        if last:
+            rise_zero = refs.pop(0)
+        refs = refs[2:]
+    inserted, crossed = refs[:2]
+    refs = refs[2:]
+    edge_out = rise_out = None
+    if not last:
+        edge_out = refs.pop(0)
+        if first:
+            rise_out = refs.pop(0)
+    rise, edge, coef = refs
+    step = pl.program_id(0)
+    steps = end - begin
+    slot = jnp.minimum(lax.rem(step, steps), 1) if last and first else jnp.int32(0)
+    turn = lax.rem(step, 2)
+
+    if not first:
+
+        @pl.when(step == 0)
+        def _():
+            edge[1, 0:HALF] = edge_in[...]
+
+    @pl.when(step < steps)
+    def _():
+        z_planes(links, later, above, staples, rise.at[slot], edge.at[turn])
+
+    if not last:
+
+        @pl.when(step == steps - 1)
+        def _():
+            edge_out[...] = edge[turn, 0:HALF]
+
+        if first:
+
+            @pl.when(step == 0)
+            def _():
+                rise_out[...] = rise[0]
+
+    if last and not first:
+
+        @pl.when(step == steps)
+        def _():
+            rise[0] = rise_zero[...]
+
+    @pl.when(step > 0 if first else step >= 0)
+    def _():
+        coefficients(flat, rise.at[slot], edge.at[1 - turn], coef)
+        insert_slice(coef, plain, inserted, crossed)
 
 
 def project_kernel(sources, crossed, sink, wave_y, wave_x, turn, owner, out, density):
     count = sources * LT * LX
 
-    def body(time, carry):
-        rows = rows_of(time)
+    step = pl.program_id(0)
+    for inner in range(sink.shape[0] // 2):
+        rows = slice(inner * LX, (inner + 1) * LX)
+        time = step * (sink.shape[0] // 2) + inner
         for source in range(sources):
             total_re = total_im = None
             for spin in range(4):
@@ -319,10 +410,10 @@
                     eta = []
                     for part in (0, 1):
                         line = (((source * 2 + part) * 4) + spin) * 3 + color
+                        lines = slice(line * 8, line * 8 + 8)
                         eta.append(
                             jnp.concatenate(
-                                [sink[2 * time + half, pl.ds(line * 8, 8), :] for half in (0, 1)],
-                                axis=0,
+                                [sink[2 * inner + half, lines, :] for half in (0, 1)], axis=0
                             ).astype(F32)
                         )
                     w_re = crossed[source, 0, spin, color, rows, :]
@@ -334,9 +425,14 @@
             place = pl.multiple_of(source * TX + time * LX, LX)
             density[pl.ds(place, LX), :] = total_re
             density[pl.ds(pl.multiple_of(count + place, LX), LX), :] = total_im
-        return carry
-
-    lax.fori_loop(0, LT, body, 0)
+
+    @pl.when(step == pl.num_programs(0) - 1)
+    def _():
+        project(sources, wave_y, wave_x, turn, owner, out, density)
+
+
+def project(sources, wave_y, wave_x, turn, owner, out, density):
+    count = sources * TX
     values = density[...]
     high = values.astype(BF16)
     low = (values - high.astype(F32)).astype(BF16)
@@ -364,8 +460,18 @@
         out[device] = piece.reshape(out.shape[1], LY).astype(BF16)
 
 
-def params():
-    return pltpu.CompilerParams(vmem_limit_bytes=VMEM_BYTES)
+def params(megabytes=56):
+    return pltpu.CompilerParams(vmem_limit_bytes=megabytes << 20)
+
+
+def slab_block(lead, time_of):
+    return pl.BlockSpec(
+        tuple(lead) + (LX, LY), lambda step: (0,) * len(lead) + (time_of(step), 0)
+    )
+
+
+def up_block(time_of):
+    return pl.BlockSpec((1, 2, 3, 3, LX, LY), lambda step: (2, 0, 0, 0, time_of(step), 0))
 
 
 def whole(count):
@@ -415,7 +521,7 @@
     owner = pair_owner[:, 0]
     number = jnp.arange(pairs, dtype=jnp.int32)
     earlier = (owner[:, None] == owner[None, :]) & (number[None, :] < number[:, None])
-    target = owner * SLOTS + jnp.sum(earlier.astype(jnp.int32), axis=1)
+    target = owner * PADDED + jnp.sum(earlier.astype(jnp.int32), axis=1)
     rows = jnp.arange(row_count, dtype=jnp.int32)[:, None] == target[None, :]
     return jnp.dot(rows.astype(BF16), picks.astype(BF16), preferred_element_type=F32)
 
@@ -437,28 +543,35 @@
     slab = TX // devices
     site = (TX, LY)
 
-    above = jnp.concatenate(
-        [from_behind(gauge_links[0:2], -1), from_behind(gauge_links[3:4], -1)], axis=0
-    )
+    matrices = (3, 2, 3, 3)
     own_staples = pl.pallas_call(
         staple_kernel,
-        out_shape=jax.ShapeDtypeStruct((3, 2, 3, 3) + site, BF16),
+        out_shape=[
+            jax.ShapeDtypeStruct(matrices + ((end - begin) * LX, LY), BF16)
+            for begin, end in PIECES
+        ],
         in_specs=whole(1),
-        out_specs=whole(1)[0],
-        compiler_params=params(),
-        cost_estimate=cost(6 * 216 * TX * LY, 4 << 20),
+        out_specs=whole(len(PIECES)),
+        compiler_params=params(16),
+        cost_estimate=cost(1000, 1000),
         name="staples",
     )(gauge_links)
-    staples = from_behind(own_staples, 1)
+    above, staples = [], []
+    for (begin, end), staple in zip(PIECES, own_staples):
+        level = gauge_links[:, :, :, :, begin * LX : end * LX]
+        level = jnp.concatenate([level[0:2], level[3:4]], axis=0)
+        above.append(from_behind(level, -1))
+        staples.append(from_behind(staple, 1))
 
     if slab == 8:
         spread = pl.pallas_call(
             spread_kernel,
             out_shape=jax.ShapeDtypeStruct((devices, lines * slab, LY), BF16),
-            in_specs=whole(1),
-            out_specs=whole(1)[0],
-            compiler_params=params(),
-            cost_estimate=cost(lines * TX * LY, 3 << 20),
+            grid=(4,),
+            in_specs=[pl.BlockSpec((lines, slab, devices // 4 * LY), lambda step: (0, 0, step))],
+            out_specs=pl.BlockSpec((devices // 4, lines * slab, LY), lambda step: (step, 0, 0)),
+            compiler_params=params(8),
+            cost_estimate=cost(1000, 1000),
             name="spread",
         )(sink_cotangent.reshape(lines, slab, devices * LY))
     else:
@@ -481,44 +594,106 @@
         in_specs=whole(1),
         out_specs=whole(1)[0],
         scratch_shapes=[pltpu.VMEM((2, 2, 3, 3) + site, F32)],
-        compiler_params=params(),
-        cost_estimate=cost(18 * 200 * TX * LY, 4 << 20),
+        compiler_params=params(16),
+        cost_estimate=cost(1000, 1000),
         name="flat_planes",
     )(gauge_links)
 
-    inserted, crossed = pl.pallas_call(
-        insert_kernel,
-        out_shape=(
+    spinors = propagators.shape[:4]
+
+    inserted = crossed = edge = rise_zero = None
+    for index, (begin, end) in enumerate(PIECES):
+        first, last = begin == 0, end == LT
+
+        def now(step):
+            return lax.rem(begin + step, LT)
+
+        def own(step):
+            return jnp.minimum(step, end - begin - 1)
+
+        def later(step):
+            return lax.rem(begin + step + 1, LT)
+
+        def written(step):
+            return lax.rem(begin + (jnp.maximum(step, 1) if first else step), LT)
+
+        operands = [gauge_links, gauge_links, above[index], staples[index], flat, propagators]
+        specs = [
+            slab_block((4, 2, 3, 3), now),
+            up_block(later),
+            slab_block(matrices, own),
+            slab_block(matrices, own),
+            slab_block((3 * HALF,), now),
+            slab_block(spinors, now),
+        ]
+        shapes = [
             jax.ShapeDtypeStruct(propagators.shape, BF16),
             jax.ShapeDtypeStruct(propagators.shape, F32),
-        ),
-        in_specs=whole(5),
-        out_specs=tuple(whole(2)),
-        scratch_shapes=[pltpu.VMEM((3 * HALF,) + site, F32), pltpu.VMEM((HALF,) + site, F32)],
-        compiler_params=params(),
-        cost_estimate=cost(5000 * TX * LY, 12 << 20),
-        name="insertion",
-    )(gauge_links, above, staples, flat, propagators)
+        ]
+        out_specs = [slab_block(spinors, written), slab_block(spinors, written)]
+        aliases = {}
+        if not first:
+            operands.append(edge)
+            specs += whole(1)
+            if last:
+                operands.append(rise_zero)
+                specs += whole(1)
+            aliases = {len(operands): 0, len(operands) + 1: 1}
+            operands += [inserted, crossed]
+            specs += [pl.BlockSpec(memory_space=pl.ANY)] * 2
+        if not last:
+            shapes.append(jax.ShapeDtypeStruct((HALF, LX, LY), F32))
+            out_specs += whole(1)
+            if first:
+                shapes.append(jax.ShapeDtypeStruct((3 * HALF, LX, LY), F32))
+                out_specs += whole(1)
+        results = pl.pallas_call(
+            functools.partial(insert_kernel, begin, end),
+            grid=(end - begin + last,),
+            out_shape=shapes,
+            in_specs=specs,
+            out_specs=out_specs,
+            input_output_aliases=aliases,
+            scratch_shapes=[
+                pltpu.VMEM((2, 3 * HALF, LX, LY), F32),
+                pltpu.VMEM((2, 2 * HALF, LX, LY), F32),
+                pltpu.VMEM((2, HALF + 18, LX, LY), F32),
+            ],
+            compiler_params=params(),
+            cost_estimate=cost(10**12, 1000),
+            name="insertion",
+        )(*operands)
+        inserted, crossed = results[:2]
+        if not last:
+            edge = results[2]
+            if first:
+                rise_zero = results[3]
 
     table_y, table_x = wave_tables()
     turn = turn_table(source_place, lax.axis_index("space"), devices)
     owner = owner_table(
-        source_time, pair_source, pair_separation, pair_owner, devices * SLOTS
+        source_time, pair_source, pair_separation, pair_owner, devices * PADDED
     )
+    steps = 4
     rows = pl.pallas_call(
         functools.partial(project_kernel, sources),
-        out_shape=jax.ShapeDtypeStruct((devices * SLOTS, 2 * NMOM), F32),
-        in_specs=whole(6),
+        grid=(steps,),
+        out_shape=jax.ShapeDtypeStruct((devices * PADDED, 2 * NMOM), F32),
+        in_specs=[
+            pl.BlockSpec(spinors + (TX // steps, LY), lambda step: (0, 0, 0, 0, step, 0)),
+            pl.BlockSpec((TX // 8 // steps, lines * 8, LY), lambda step: (step, 0, 0)),
+        ]
+        + whole(4),
         out_specs=whole(1)[0],
         scratch_shapes=[pltpu.VMEM((2 * sources * TX, LY), F32)],
         compiler_params=params(),
-        cost_estimate=cost(300 * TX * LY, 5 << 20),
+        cost_estimate=cost(1000, 1000),
         name="projection",
     )(crossed, sink, jnp.asarray(table_y), jnp.asarray(table_x), turn, owner)
     parts = lax.all_to_all(
-        rows.reshape(devices, SLOTS, 2 * NMOM), "space", split_axis=0, concat_axis=0, tiled=True
+        rows.reshape(devices, PADDED, 2 * NMOM), "space", split_axis=0, concat_axis=0, tiled=True
     )
-    return inserted, jnp.sum(parts, axis=0)
+    return inserted, jnp.sum(parts[:, :SLOTS], axis=0)
 
 
 def solution(mesh):

time: 105 us -> 89.9 us (0.86)
  waiting for transfers between devices: 20.8 us -> 11.3 us
  Pallas kernels: 40.8 us -> 33.7 us
  starting transfers between devices: 12.3 us -> 15.7 us
  blocking collectives: 20.6 us -> 18.7 us
    ppermute x3 -> x4, waiting for transfers between devices: 20.8 us -> 0.01 us  [from_behind(): lax.ppermute(block, 'space', [((i - distance) % count, i) for i in range(...]
    all_to_all x1, waiting for transfers between devices: 0.01 us -> 11.3 us  [on_device(): lax.all_to_all(spread, 'space', split_axis=0, concat_axis=0, tiled=True)]
    ppermute x3 -> x4, starting transfers between devices: 4.9 us -> 9.86 us  [from_behind(): lax.ppermute(block, 'space', [((i - distance) % count, i) for i in range(...]
    pallas_call x1, Pallas kernels: 12 us -> 9.17 us  [on_device(): pl.pallas_call(flat_kernel, out_shape=jax.ShapeDtypeStruct((3 * HALF,) +...]
    pallas_call x1, Pallas kernels: 2.83 us -> 0.46 us  [on_device(): pl.pallas_call(spread_kernel, out_shape=jax.ShapeDtypeStruct((devices, li...]
    pallas_call x3 -> x4, Pallas kernels: 26 us -> 24 us  [the longest x2 15.4 us: on_device(): pl.pallas_call(functools.partial(insert_kernel, begin, end), grid=(end -...]
    all_to_all x1, blocking collectives: 20.6 us -> 18.7 us  [on_device(): lax.all_to_all(rows.reshape(devices, PADDED, 2 * NMOM), 'space', split_ax...]
    unnamed x12 -> x24, local copies, waits for them, and re-layouts: 1.24 us -> 2.92 us
  transfers between devices with their start and end apart: 4 -> 5, of which waited for: 3 -> 1; matrix products, arithmetic and copies ran while one was open for 6% -> 3% of each run, Pallas kernels for 32% -> 32%
where the time goes in v1:
time: 89.9 us; the launch traced here: 89.4 us
  Pallas kernels  33.7 us (37%)
  blocking collectives  18.7 us (21%)
  starting transfers between devices  15.7 us (17%)
  waiting for transfers between devices  11.3 us (13%)
  local copies, waits for them, and re-layouts  5.08 us (6%)
  other arithmetic  3.23 us (4%)
    all_to_all x1, blocking collectives, on_device(): lax.all_to_all(rows.reshape(devices, PADDED, 2 * NMOM), 'space', split_ax...  18.7 us
    pallas_call x2, Pallas kernels, on_device(): pl.pallas_call(functools.partial(insert_kernel, begin, end), grid=(end -...  15.4 us
    all_to_all x1, waiting for transfers between devices, on_device(): lax.all_to_all(spread, 'space', split_axis=0, concat_axis=0, tiled=True)  11.3 us
    ppermute x4, starting transfers between devices, from_behind(): lax.ppermute(block, 'space', [((i - distance) % count, i) for i in range(...  9.86 us
    pallas_call x1, Pallas kernels, on_device(): pl.pallas_call(flat_kernel, out_shape=jax.ShapeDtypeStruct((3 * HALF,) +...  9.17 us
    all_to_all x1, starting transfers between devices, on_device(): lax.all_to_all(spread, 'space', split_axis=0, concat_axis=0, tiled=True)  5.86 us
    pallas_call x1, Pallas kernels, on_device(): pl.pallas_call(functools.partial(project_kernel, sources), grid=(steps,),...  4.82 us
    pallas_call x1, Pallas kernels, on_device(): pl.pallas_call(staple_kernel, out_shape=[jax.ShapeDtypeStruct(matrices +...  3.87 us
  transfers between devices with their start and end apart: 5, of which 1 were waited for; matrix products, arithmetic and copies ran while one was open for 3% of the time, Pallas kernels for 32%

profile of v1, /device:TPU:0, one launch (start us, length us, event | category | flops | bytes accessed | tf_op | source)
XLA Modules:
  0.0 89.4 jit_solution(10483797065910591063)
XLA Ops:
  0.6 0.0 copy-start
  0.6 1.5 %fusion.21 = (bf16[2,2,3,3,64,128]{5,4,3,2,1,0:T(8,128)(2,1)S(1)}, bf16[2,2,3,3,64,128]{5,4,3,2,1,0:T(8,128)(2,1)S(1)}) fusion(bf16[4,2,3,3,128,128]{5,4,3,2,1,0:T(8,128)(2,1)} %refs_1_.3), kind=kLoop, calls=%fused_computation.50 | loop fusion | bytes 2359296 | tf_op jit(solution)/shard_map/slice | solution.py:562
  2.2 0.5 copy-done
  2.7 1.0 %pad_maximum_fusion.1 = bf16[3,2,3,3,64,128]{5,4,3,2,1,0:T(8,128)(2,1)} fusion(bf16[1,2,3,3,64,128]{5,4,3,2,1,0:T(8,128)(2,1)S(1)} %get-tuple-element.23, bf16[2,2,3,3,64,128]{5,4,3,2,1,0:T(8,128)(2,1)S(1)} %get-tuple-element.21), kind=kLoop, calls=%fused_computation.1 | loop fusion | flops 442368 | bytes 1769472 | tf_op jit(solution)/shard_map/concatenate | solution.py:562
  3.7 0.0 copy-start.3
  3.7 5.4 %collective-permute-start.2 = (bf16[3,2,3,3,64,128]{5,4,3,2,1,0:T(8,128)(2,1)}, bf16[3,2,3,3,64,128]{5,4,3,2,1,0:T(8,128)(2,1)}, u32[]{:S(2)}, u32[]{:S(2)}) collective-permute-start(bf16[3,2,3,3,64,128]{5,4,3,2,1,0:T(8,128)(2,1)} %pad_maximum_fusion.1), channel_id=1, source_target_pairs={{1,0},{2,1},{3,2},{4,3},{5,4},{6,5},{7,6},{8,7},{9,8},{10,9},{11,1... | collective-permute-start | bytes 2654216 | tf_op jit(solution)/shard_map/ppermute | solution.py:31
  9.1 3.9 %staples.1 = (bf16[3,2,3,3,64,128]{5,4,3,2,1,0:T(8,128)(2,1)S(1)}, bf16[3,2,3,3,64,128]{5,4,3,2,1,0:T(8,128)(2,1)}) custom-call(bf16[4,2,3,3,128,128]{5,4,3,2,1,0:T(8,128)(2,1)S(1)} %copy-done), custom_call_target="tpu_custom_call" | custom-call | flops 1000 | bytes 1000 | tf_op jit(solution)/shard_map/staples/pallas_call | solution.py:547
  13.0 0.0 collective-permute-start.3
  13.0 1.0 %pad_maximum_fusion = bf16[3,2,3,3,64,128]{5,4,3,2,1,0:T(8,128)(2,1)} fusion(bf16[1,2,3,3,64,128]{5,4,3,2,1,0:T(8,128)(2,1)S(1)} %get-tuple-element.24, bf16[2,2,3,3,64,128]{5,4,3,2,1,0:T(8,128)(2,1)S(1)} %get-tuple-element.22), kind=kLoop, calls=%fused_computation | loop fusion | flops 442368 | bytes 1769472 | tf_op jit(solution)/shard_map/concatenate | solution.py:562
  14.0 4.4 %collective-permute-start = (bf16[3,2,3,3,64,128]{5,4,3,2,1,0:T(8,128)(2,1)}, bf16[3,2,3,3,64,128]{5,4,3,2,1,0:T(8,128)(2,1)}, u32[]{:S(2)}, u32[]{:S(2)}) collective-permute-start(bf16[3,2,3,3,64,128]{5,4,3,2,1,0:T(8,128)(2,1)} %pad_maximum_fusion), channel_id=1, source_target_pairs={{1,0},{2,1},{3,2},{4,3},{5,4},{6,5},{7,6},{8,7},{9,8},{10,9},{11,1... | collective-permute-start | bytes 2654216 | tf_op jit(solution)/shard_map/ppermute | solution.py:31
  18.5 0.0 collective-permute-start.1
  18.5 0.0 copy-done.3
  18.5 0.5 spread.1
  18.9 0.0 copy-start.1
  18.9 1.2 %copy-done.1 = bf16[16,384,128]{2,1,0:T(8,128)(2,1)} copy-done((bf16[16,384,128]{2,1,0:T(8,128)(2,1)}, bf16[16,384,128]{2,1,0:T(8,128)(2,1)S(1)}, u32[]{:S(2)}) %copy-start.1) | copy-done | bytes 1572888
  20.1 5.9 %all-to-all-start = ((bf16[16,384,128]{2,1,0:T(8,128)(2,1)}), bf16[16,384,128]{2,1,0:T(8,128)(2,1)}, u32[]{:S(2)}, u32[]{:S(2)}) async-start(bf16[16,384,128]{2,1,0:T(8,128)(2,1)} %copy-done.1), calls=%async_computation | async-start | bytes 3145728 | tf_op jit(solution)/shard_map/all_to_all | solution.py:583
  26.0 0.0 copy-start.7
  26.0 0.0 copy-start.4
  26.0 0.0 copy-start.8
  26.0 0.0 copy-start.9
  26.0 0.0 copy-start.10
  26.0 0.0 copy-start.5
  26.0 0.0 copy-start.11
  26.1 0.0 copy-start.6
  26.1 9.2 %flat_planes.1.refs_4_ = f32[27,128,128]{2,1,0:T(8,128)S(1)} custom-call(bf16[4,2,3,3,128,128]{5,4,3,2,1,0:T(8,128)(2,1)S(1)} %copy-done), custom_call_target="tpu_custom_call" | custom-call | flops 1000 | bytes 1000 | tf_op jit(solution)/shard_map/flat_planes/pallas_call | solution.py:591
  35.2 0.0 copy-start.2
  35.3 1.2 %copy-done.2 = f32[27,128,128]{2,1,0:T(8,128)} copy-done((f32[27,128,128]{2,1,0:T(8,128)}, f32[27,128,128]{2,1,0:T(8,128)S(1)}, u32[]{:S(2)}) %copy-start.2) | copy-done | bytes 1769496
  36.5 0.0 copy-done.7
  36.5 0.2 convert_reduce_fusion
  36.6 0.0 copy-done.4
  36.7 0.2 slice_reduce_fusion.2
  36.8 0.0 copy-done.8
  36.8 0.0 copy-done.9
  36.9 0.0 copy-done.10
  36.9 0.1 fusion.20
  37.0 0.0 copy-done.5
  37.0 0.0 copy-done.11
  37.0 0.1 fusion.16
  37.1 0.0 copy-done.6
  37.1 0.6 broadcast_bitcast_fusion.turn
  37.7 0.8 fusion.owner
  38.6 0.0 collective-permute-done.2.refs_2_
  38.6 0.0 collective-permute-done.3.refs_3_
  38.6 7.1 %insertion.2 = (bf16[2,2,4,3,128,128]{5,4,3,2,1,0:T(8,128)(2,1)}, f32[2,2,4,3,128,128]{5,4,3,2,1,0:T(8,128)}, f32[9,16,128]{2,1,0:T(8,128)}, f32[27,16,128]{2,1,0:T(8,128)}) custom-call(bf16[4,2,3,3,128,128]{5,4,3,2,1,0:T(8,128)(2,1)} %refs_1_.3, bf16[4,2,3,3,128,128]{5,4,3,2,1,0:T(8,128)(2,1)} %refs_1_.3, ...), custom_call_target="tpu_custom_call" | custom-call | flops 999999995904 | bytes 1000 | tf_op jit(solution)/shard_map/insertion/pallas_call | solution.py:650
  45.7 0.0 collective-permute-done.refs_2_
  45.7 0.0 collective-permute-done.1.refs_3_
  45.7 8.3 %insertion.3 = (bf16[2,2,4,3,128,128]{5,4,3,2,1,0:T(8,128)(2,1)}, f32[2,2,4,3,128,128]{5,4,3,2,1,0:T(8,128)}) custom-call(bf16[4,2,3,3,128,128]{5,4,3,2,1,0:T(8,128)(2,1)} %refs_1_.3, bf16[4,2,3,3,128,128]{5,4,3,2,1,0:T(8,128)(2,1)} %refs_1_.3, ...), custom_call_target="tpu_custom_call", output_to_operand_aliasing={{0}: (8, {}), {1}: (9, {})} | custom-call | flops 999999995904 | bytes 1000 | tf_op jit(solution)/shard_map/insertion/pallas_call | solution.py:650
  53.9 11.3 %all-to-all-done.sink = bf16[16,384,128]{2,1,0:T(8,128)(2,1)} async-done(((bf16[16,384,128]{2,1,0:T(8,128)(2,1)}), bf16[16,384,128]{2,1,0:T(8,128)(2,1)}, u32[]{:S(2)}, u32[]{:S(2)}) %all-to-all-start) | async-done | bytes 1572896 | tf_op jit(solution)/shard_map/all_to_all | solution.py:583
  65.3 4.8 %projection.1 = f32[128,256]{1,0:T(8,128)} custom-call(f32[2,2,4,3,128,128]{5,4,3,2,1,0:T(8,128)} %get-tuple-element.17.crossed, bf16[16,384,128]{2,1,0:T(8,128)(2,1)} %all-to-all-done.sink, bf16[2,128,256]{2,1,0:T(8,128)(2,1)} %constant.77.clone.wave_y, f32[2,16,128]{2,1,0:T(8,128)} %constant.78.clone.wave_x, f32[2,16,128]{2,1,0:T(8,128)} %broadcast_bitcast_fusion.turn, ...), custom_call_target="tpu_custom_call" | custom-call | flops 1000 | bytes 1000 | tf_op jit(solution)/shard_map/projection/pallas_call | solution.py:678
  70.1 18.7 %all_to_all.10 = f32[16,8,256]{2,1,0:T(8,128)S(1)} all-to-all(f32[16,8,256]{2,1,0:T(8,128)} %bitcast.7), channel_id=1, replica_groups=mesh['grp'=2,'space'=16] {'space'}, dimensions={0} | all-to-all | bytes 262144 | tf_op jit(solution)/shard_map/all_to_all | solution.py:693
  88.8 0.6 slice_reduce_fusion
  (3 shorter events, 0.1 us)
Async XLA Ops:
  0.6 2.0 %copy-start = (bf16[4,2,3,3,128,128]{5,4,3,2,1,0:T(8,128)(2,1)S(1)}, bf16[4,2,3,3,128,128]{5,4,3,2,1,0:T(8,128)(2,1)}, u32[]{:S(2)}) copy-start(bf16[4,2,3,3,128,128]{5,4,3,2,1,0:T(8,128)(2,1)} %refs_1_.3) | copy-start | bytes 7077892
  3.7 14.8 %copy-start.3 = (bf16[2,2,4,3,8,2048]{5,4,3,2,1,0:T(8,128)(2,1)S(1)}, bf16[2,2,4,3,8,2048]{5,4,3,2,1,0:T(8,128)(2,1)}, u32[]{:S(2)}) copy-start(bf16[2,2,4,3,8,2048]{5,4,3,2,1,0:T(8,128)(2,1)} %param.15) | copy-start | bytes 4718596
  3.7 34.9 %collective-permute-start.2 = (bf16[3,2,3,3,64,128]{5,4,3,2,1,0:T(8,128)(2,1)}, bf16[3,2,3,3,64,128]{5,4,3,2,1,0:T(8,128)(2,1)}, u32[]{:S(2)}, u32[]{:S(2)}) collective-permute-start(bf16[3,2,3,3,64,128]{5,4,3,2,1,0:T(8,128)(2,1)} %pad_maximum_fusion.1), channel_id=1, source_target_pairs={{1,0},{2,1},{3,2},{4,3},{5,4},{6,5},{7,6},{8,7},{9,8},{10,9},{11,1... | collective-permute-start | bytes 2654216 | tf_op jit(solution)/shard_map/ppermute | solution.py:31
  13.0 25.6 %collective-permute-start.3 = (bf16[3,2,3,3,64,128]{5,4,3,2,1,0:T(8,128)(2,1)S(1)}, bf16[3,2,3,3,64,128]{5,4,3,2,1,0:T(8,128)(2,1)}, u32[]{:S(2)}, u32[]{:S(2)}) collective-permute-start(bf16[3,2,3,3,64,128]{5,4,3,2,1,0:T(8,128)(2,1)S(1)} %get-tuple-element.11), channel_id=1, source_target_pairs={{15,0},{0,1},{1,2},{2,3},{3,4},{4,5},{5,6},{6,7},{7,8},{8,9},{9,10... | collective-permute-start | bytes 2654216 | tf_op jit(solution)/shard_map/ppermute | solution.py:31
  14.0 31.6 %collective-permute-start = (bf16[3,2,3,3,64,128]{5,4,3,2,1,0:T(8,128)(2,1)}, bf16[3,2,3,3,64,128]{5,4,3,2,1,0:T(8,128)(2,1)}, u32[]{:S(2)}, u32[]{:S(2)}) collective-permute-start(bf16[3,2,3,3,64,128]{5,4,3,2,1,0:T(8,128)(2,1)} %pad_maximum_fusion), channel_id=1, source_target_pairs={{1,0},{2,1},{3,2},{4,3},{5,4},{6,5},{7,6},{8,7},{9,8},{10,9},{11,1... | collective-permute-start | bytes 2654216 | tf_op jit(solution)/shard_map/ppermute | solution.py:31
  18.5 27.2 %collective-permute-start.1 = (bf16[3,2,3,3,64,128]{5,4,3,2,1,0:T(8,128)(2,1)}, bf16[3,2,3,3,64,128]{5,4,3,2,1,0:T(8,128)(2,1)}, u32[]{:S(2)}, u32[]{:S(2)}) collective-permute-start(bf16[3,2,3,3,64,128]{5,4,3,2,1,0:T(8,128)(2,1)} %get-tuple-element.10), channel_id=1, source_target_pairs={{15,0},{0,1},{1,2},{2,3},{3,4},{4,5},{5,6},{6,7},{7,8},{8,9},{9,10... | collective-permute-start | bytes 2654216 | tf_op jit(solution)/shard_map/ppermute | solution.py:31
  18.9 1.2 %copy-start.1 = (bf16[16,384,128]{2,1,0:T(8,128)(2,1)}, bf16[16,384,128]{2,1,0:T(8,128)(2,1)S(1)}, u32[]{:S(2)}) copy-start(bf16[16,384,128]{2,1,0:T(8,128)(2,1)S(1)} %spread.1) | copy-start | bytes 4718596
  20.1 45.2 %all-to-all-start = ((bf16[16,384,128]{2,1,0:T(8,128)(2,1)}), bf16[16,384,128]{2,1,0:T(8,128)(2,1)}, u32[]{:S(2)}, u32[]{:S(2)}) async-start(bf16[16,384,128]{2,1,0:T(8,128)(2,1)} %copy-done.1), calls=%async_computation | async-start | bytes 3145728 | tf_op jit(solution)/shard_map/all_to_all | solution.py:583
  26.0 10.5 %copy-start.7 = (s32[32,1]{0,1:T(1,128)S(1)}, s32[32,1]{0,1:T(1,128)}, u32[]{:S(2)}) copy-start(s32[32,1]{0,1:T(1,128)} %param.20) | copy-start | bytes 388
  26.0 10.7 %copy-start.4 = (s32[2,3]{1,0:T(2,128)S(1)}, s32[2,3]{1,0:T(2,128)}, u32[]{:S(2)}) copy-start(s32[2,3]{1,0:T(2,128)} %param.17) | copy-start | bytes 76
  26.0 10.8 %copy-start.8 = (s32[128]{0:T(128)S(1)}, s32[128]{0:T(128)}, u32[]{:S(2)}) copy-start(s32[128]{0:T(128)} %constant.74.clone) | copy-start | bytes 1540
  26.0 10.8 %copy-start.9 = (s32[128]{0:T(128)S(1)}, s32[128]{0:T(128)}, u32[]{:S(2)}) copy-start(s32[128]{0:T(128)} %constant.75.clone) | copy-start | bytes 1540
  26.0 10.8 %copy-start.10 = (s32[128]{0:T(128)S(1)}, s32[128]{0:T(128)}, u32[]{:S(2)}) copy-start(s32[128]{0:T(128)} %constant.76.clone) | copy-start | bytes 1540
  26.0 11.0 %copy-start.5 = (s32[32]{0:T(128)S(1)}, s32[32]{0:T(128)}, u32[]{:S(2)}) copy-start(s32[32]{0:T(128)} %param.18) | copy-start | bytes 388
  26.0 11.0 %copy-start.11 = (s32[2]{0:T(128)S(1)}, s32[2]{0:T(128)}, u32[]{:S(2)}) copy-start(s32[2]{0:T(128)} %param.16) | copy-start | bytes 28
  26.1 11.1 %copy-start.6 = (s32[32]{0:T(128)S(1)}, s32[32]{0:T(128)}, u32[]{:S(2)}) copy-start(s32[32]{0:T(128)} %param.19) | copy-start | bytes 388
  35.2 1.2 %copy-start.2 = (f32[27,128,128]{2,1,0:T(8,128)}, f32[27,128,128]{2,1,0:T(8,128)S(1)}, u32[]{:S(2)}) copy-start(f32[27,128,128]{2,1,0:T(8,128)S(1)} %flat_planes.1.refs_4_) | copy-start | bytes 5308420

commit v2 on v1

--- a/solution.py
+++ b/solution.py
@@ -18,7 +18,7 @@
 OUTPUT_SCALE = 0.1
 F32 = jnp.float32
 BF16 = jnp.bfloat16
-PIECES = ((0, 4), (4, 8))
+PIECES = ((0, 5), (5, 8))
 PADDED = 8
 UPPER = ((0, 1), (0, 2), (1, 2))
 SYMMETRIC = ((0, 0), (1, 1), (2, 2), (0, 1), (0, 2), (1, 2))
@@ -106,6 +106,13 @@
     return [[tuple(load(part, i, j) for part in (0, 1)) for j in range(3)] for i in range(3)]
 
 
+def load_line(ref, slot, half):
+    def load(part, i, j):
+        return ref[0, ((slot * 2 + part) * 3 + i) * 3 + j].astype(F32)[half]
+
+    return [[tuple(load(part, i, j) for part in (0, 1)) for j in range(3)] for i in range(3)]
+
+
 def halved(matrix, half):
     return mapped(lambda value: value[half], matrix)
 
@@ -132,22 +139,21 @@
     return mapped(up_x if step == 0 else up_y, load_matrix(ref, direction, time))
 
 
-def staple_kernel(links, *outs):
-    def body(out, begin, step, carry):
+def staple_kernel(begin, level, upward, out):
+    def body(step, carry):
         time = begin + step
-        rows = rows_of(step)
-        up_link = load_matrix(links, 2, time)
-        for slot, direction in enumerate((0, 1, 3)):
-            left = product(up_link, load_matrix(links, direction, time), left_dagger=True)
-            staple = product(left, neighbour_link(links, 2, direction, time))
+        up_link = load_matrix(upward, 0, time)
+        for slot in range(3):
+            left = product(up_link, load_matrix(level, slot, step), left_dagger=True)
+            direction = (0, 1, 3)[slot]
+            staple = product(left, neighbour_link(upward, 0, direction, time))
             for i in range(3):
                 for j in range(3):
                     for part in (0, 1):
-                        out[slot, part, i, j, rows, :] = staple[i][j][part].astype(BF16)
+                        out[step, ((slot * 2 + part) * 3 + i) * 3 + j] = staple[i][j][part].astype(BF16)
         return carry
 
-    for out, (begin, end) in zip(outs, PIECES):
-        lax.fori_loop(0, end - begin, functools.partial(body, out, jnp.int32(begin)), 0)
+    lax.fori_loop(0, out.shape[0], body, 0)
 
 
 def flat_kernel(links, out, corner):
@@ -167,7 +173,6 @@
     lax.fori_loop(0, LT, lower, 0)
 
     def upper(time, carry):
-        rows = rows_of(time)
         for slot, direction in enumerate((0, 1)):
             far = product(
                 load_matrix(links, 3, time), neighbour_link(links, direction, 3, time)
@@ -179,7 +184,7 @@
             behind = anti_product(bend, link)
             move = down_x if direction == 0 else down_y
             for index in range(HALF):
-                out[(slot + 1) * HALF + index, rows, :] = ahead[index] + move(behind[index])
+                out[time, (slot + 1) * HALF + index] = ahead[index] + move(behind[index])
         link_x, link_y = load_matrix(links, 0, time), load_matrix(links, 1, time)
         over_x, over_y = mapped(up_y, link_x), mapped(up_x, link_y)
         near = product(link_x, product(link_y, over_x), left_dagger=True)
@@ -188,7 +193,7 @@
         ahead = anti_product(link_y, bend)
         behind = anti_product(bend, link_y)
         for index in range(HALF):
-            out[index, rows, :] = -(ahead[index] + down_y(behind[index]))
+            out[time, index] = -(ahead[index] + down_y(behind[index]))
         return carry
 
     lax.fori_loop(0, LT, upper, 0)
@@ -207,7 +212,7 @@
             far = product(up_link, load_matrix(above, slot, 0, half))
             moved = halved(neighbour_up(links, later, direction), half)
             far = product(moved, far, right_dagger=True)
-            bend = minus_adjoint(far, load_matrix(staples, slot, 0, half))
+            bend = minus_adjoint(far, load_line(staples, slot, half))
             link = load_matrix(links, direction, 0, half)
             for index, value in enumerate(anti_product(link, bend)):
                 rise[slot * HALF + index, half, :] = value
@@ -331,10 +336,10 @@
                 for a, b, c in ((0, 1, 2), (1, 2, 0), (2, 0, 1)):
                     (a_re, a_im), (b_re, b_im) = result[a], result[b]
                     (p_re, p_im), (q_re, q_im) = vector[a], vector[b]
-                    crossed[source, 0, 2 * block + spin, c] = (
+                    crossed[0, ((source * 2) * 4 + 2 * block + spin) * 3 + c] = (
                         a_re * q_re - a_im * q_im - b_re * p_re + b_im * p_im
                     )
-                    crossed[source, 1, 2 * block + spin, c] = (
+                    crossed[0, ((source * 2 + 1) * 4 + 2 * block + spin) * 3 + c] = (
                         a_re * q_im + a_im * q_re - b_re * p_im - b_im * p_re
                     )
 
@@ -392,7 +397,7 @@
 
     @pl.when(step > 0 if first else step >= 0)
     def _():
-        coefficients(flat, rise.at[slot], edge.at[1 - turn], coef)
+        coefficients(flat.at[0], rise.at[slot], edge.at[1 - turn], coef)
         insert_slice(coef, plain, inserted, crossed)
 
 
@@ -401,7 +406,6 @@
 
     step = pl.program_id(0)
     for inner in range(sink.shape[0] // 2):
-        rows = slice(inner * LX, (inner + 1) * LX)
         time = step * (sink.shape[0] // 2) + inner
         for source in range(sources):
             total_re = total_im = None
@@ -413,11 +417,12 @@
                         lines = slice(line * 8, line * 8 + 8)
                         eta.append(
                             jnp.concatenate(
-                                [sink[2 * inner + half, lines, :] for half in (0, 1)], axis=0
-                            ).astype(F32)
+                                [sink[2 * inner + half, lines, :].astype(F32) for half in (0, 1)],
+                                axis=0,
+                            )
                         )
-                    w_re = crossed[source, 0, spin, color, rows, :]
-                    w_im = crossed[source, 1, spin, color, rows, :]
+                    w_re = crossed[inner, ((source * 2) * 4 + spin) * 3 + color]
+                    w_im = crossed[inner, ((source * 2 + 1) * 4 + spin) * 3 + color]
                     re = w_re * eta[0] - w_im * eta[1]
                     im = w_re * eta[1] + w_im * eta[0]
                     total_re = re if total_re is None else total_re + re
@@ -454,6 +459,24 @@
     )
 
 
+def pack_kernel(links, *refs):
+    outs, upward, sems = refs[: len(PIECES)], refs[len(PIECES)], refs[-1]
+    copies = []
+    for index, (out, (begin, end)) in enumerate(zip(outs, PIECES)):
+        rows = slice(begin * LX, end * LX)
+        for part, (place, source) in enumerate(((slice(0, 2), slice(0, 2)), (slice(2, 3), slice(3, 4)))):
+            copies.append(
+                pltpu.make_async_copy(
+                    links.at[source, :, :, :, rows], out.at[place], sems.at[2 * index + part]
+                )
+            )
+    copies.append(pltpu.make_async_copy(links.at[2:3], upward, sems.at[2 * len(PIECES)]))
+    for copy in copies:
+        copy.start()
+    for copy in copies:
+        copy.wait()
+
+
 def spread_kernel(sink, out):
     for device in range(out.shape[0]):
         piece = sink[:, :, device * LY : (device + 1) * LY].astype(F32)
@@ -544,24 +567,34 @@
     site = (TX, LY)
 
     matrices = (3, 2, 3, 3)
-    own_staples = pl.pallas_call(
-        staple_kernel,
+    *levels, upward = pl.pallas_call(
+        pack_kernel,
         out_shape=[
             jax.ShapeDtypeStruct(matrices + ((end - begin) * LX, LY), BF16)
             for begin, end in PIECES
-        ],
-        in_specs=whole(1),
-        out_specs=whole(len(PIECES)),
-        compiler_params=params(16),
+        ]
+        + [jax.ShapeDtypeStruct((1, 2, 3, 3) + site, BF16)],
+        in_specs=[pl.BlockSpec(memory_space=pl.ANY)],
+        out_specs=whole(len(PIECES) + 1),
+        scratch_shapes=[pltpu.SemaphoreType.DMA((2 * len(PIECES) + 1,))],
+        compiler_params=params(6),
         cost_estimate=cost(1000, 1000),
-        name="staples",
+        name="pack",
     )(gauge_links)
-    above, staples = [], []
-    for (begin, end), staple in zip(PIECES, own_staples):
-        level = gauge_links[:, :, :, :, begin * LX : end * LX]
-        level = jnp.concatenate([level[0:2], level[3:4]], axis=0)
-        above.append(from_behind(level, -1))
-        staples.append(from_behind(staple, 1))
+    def piece_staples(index):
+        begin, end = PIECES[index]
+        return pl.pallas_call(
+            functools.partial(staple_kernel, begin),
+            out_shape=jax.ShapeDtypeStruct((end - begin, 54, LX, LY), BF16),
+            in_specs=whole(2),
+            out_specs=whole(1)[0],
+            compiler_params=params(12),
+            cost_estimate=cost(1000, 1000),
+            name="staples",
+        )(levels[index], upward)
+
+    above = [from_behind(level, -1) for level in levels]
+    staples = [from_behind(piece_staples(0), 1)]
 
     if slab == 8:
         spread = pl.pallas_call(
@@ -588,13 +621,15 @@
             .reshape(TX // 8, lines * 8, LY)
         )
 
+    staples += [from_behind(piece_staples(index), 1) for index in range(1, len(PIECES))]
+
     flat = pl.pallas_call(
         flat_kernel,
-        out_shape=jax.ShapeDtypeStruct((3 * HALF,) + site, F32),
+        out_shape=jax.ShapeDtypeStruct((LT, 3 * HALF, LX, LY), F32),
         in_specs=whole(1),
         out_specs=whole(1)[0],
         scratch_shapes=[pltpu.VMEM((2, 2, 3, 3) + site, F32)],
-        compiler_params=params(16),
+        compiler_params=params(),
         cost_estimate=cost(1000, 1000),
         name="flat_planes",
     )(gauge_links)
@@ -622,15 +657,18 @@
             slab_block((4, 2, 3, 3), now),
             up_block(later),
             slab_block(matrices, own),
-            slab_block(matrices, own),
-            slab_block((3 * HALF,), now),
+            pl.BlockSpec((1, 54, LX, LY), lambda step: (own(step), 0, 0, 0)),
+            pl.BlockSpec((1, 3 * HALF, LX, LY), lambda step: (now(step), 0, 0, 0)),
             slab_block(spinors, now),
         ]
         shapes = [
             jax.ShapeDtypeStruct(propagators.shape, BF16),
-            jax.ShapeDtypeStruct(propagators.shape, F32),
+            jax.ShapeDtypeStruct((LT, lines, LX, LY), F32),
         ]
-        out_specs = [slab_block(spinors, written), slab_block(spinors, written)]
+        out_specs = [
+            slab_block(spinors, written),
+            pl.BlockSpec((1, lines, LX, LY), lambda step: (written(step), 0, 0, 0)),
+        ]
         aliases = {}
         if not first:
             operands.append(edge)
@@ -674,13 +712,13 @@
     owner = owner_table(
         source_time, pair_source, pair_separation, pair_owner, devices * PADDED
     )
-    steps = 4
+    steps = 2
     rows = pl.pallas_call(
         functools.partial(project_kernel, sources),
         grid=(steps,),
         out_shape=jax.ShapeDtypeStruct((devices * PADDED, 2 * NMOM), F32),
         in_specs=[
-            pl.BlockSpec(spinors + (TX // steps, LY), lambda step: (0, 0, 0, 0, step, 0)),
+            pl.BlockSpec((LT // steps, lines, LX, LY), lambda step: (step, 0, 0, 0)),
             pl.BlockSpec((TX // 8 // steps, lines * 8, LY), lambda step: (step, 0, 0)),
         ]
         + whole(4),

time: 89.9 us -> 86.7 us (0.964)
  Pallas kernels: 33.7 us -> 39.4 us
  waiting for transfers between devices: 11.3 us -> 6.33 us
  other arithmetic: 3.23 us -> 1.2 us
  local copies, waits for them, and re-layouts: 5.08 us -> 3.36 us
    pallas_call x2 -> x4, Pallas kernels: 13 us -> 18.2 us  [the longest x1 12.1 us: on_device(): pl.pallas_call(flat_kernel, out_shape=jax.ShapeDtypeStruct((LT, 3 * HALF,...]
    all_to_all x1, waiting for transfers between devices: 11.3 us -> 6.32 us  [on_device(): lax.all_to_all(spread, 'space', split_axis=0, concat_axis=0, tiled=True)]
    concatenate x2 -> x0, other arithmetic: 2.02 us -> none  [on_device(): level = jnp.concatenate([level[0:2], level[3:4]], axis=0)]
    slice x2 -> x0, local copies, waits for them, and re-layouts: 1.56 us -> none  [on_device(): level = jnp.concatenate([level[0:2], level[3:4]], axis=0)]
    pallas_call x1, Pallas kernels: 0.46 us -> 1.87 us  [on_device(): pl.pallas_call(spread_kernel, out_shape=jax.ShapeDtypeStruct((devices, li...]
    unnamed x24 -> x22, local copies, waits for them, and re-layouts: 2.92 us -> 2.76 us
  transfers between devices with their start and end apart: 5 -> 5, of which waited for: 1 -> 1; matrix products, arithmetic and copies ran while one was open for 3% -> 2% of each run, Pallas kernels for 32% -> 40%
where the time goes in v2:
time: 86.7 us; the launch traced here: 86.2 us
  Pallas kernels  39.4 us (45%)
  blocking collectives  18.3 us (21%)
  starting transfers between devices  16 us (18%)
  waiting for transfers between devices  6.33 us (7%)
  local copies, waits for them, and re-layouts  3.36 us (4%)
  other arithmetic  1.2 us (1%)
    all_to_all x1, blocking collectives, on_device(): lax.all_to_all(rows.reshape(devices, PADDED, 2 * NMOM), 'space', split_ax...  18.3 us
    pallas_call x2, Pallas kernels, on_device(): pl.pallas_call(functools.partial(insert_kernel, begin, end), grid=(end -...  15.2 us
    pallas_call x1, Pallas kernels, on_device(): pl.pallas_call(flat_kernel, out_shape=jax.ShapeDtypeStruct((LT, 3 * HALF,...  12.1 us
    ppermute x4, starting transfers between devices, from_behind(): lax.ppermute(block, 'space', [((i - distance) % count, i) for i in range(...  9.96 us
    all_to_all x1, waiting for transfers between devices, on_device(): lax.all_to_all(spread, 'space', split_axis=0, concat_axis=0, tiled=True)  6.32 us
    all_to_all x1, starting transfers between devices, on_device(): lax.all_to_all(spread, 'space', split_axis=0, concat_axis=0, tiled=True)  6.01 us
    pallas_call x2, Pallas kernels, piece_staples(): pl.pallas_call(functools.partial(staple_kernel, begin), out_shape=jax.Sha...  4.88 us
    pallas_call x1, Pallas kernels, on_device(): pl.pallas_call(functools.partial(project_kernel, sources), grid=(steps,),...  4.16 us
  transfers between devices with their start and end apart: 5, of which 1 were waited for; matrix products, arithmetic and copies ran while one was open for 2% of the time, Pallas kernels for 40%

profile of v2, /device:TPU:0, one launch (start us, length us, event | category | flops | bytes accessed | tf_op | source)
XLA Modules:
  0.0 86.2 jit_solution(17928337919559751801)
XLA Ops:
  0.6 0.0 copy-start
  0.6 1.7 %copy-done = bf16[4,2,3,3,128,128]{5,4,3,2,1,0:T(8,128)(2,1)S(1)} copy-done((bf16[4,2,3,3,128,128]{5,4,3,2,1,0:T(8,128)(2,1)S(1)}, bf16[4,2,3,3,128,128]{5,4,3,2,1,0:T(8,128)(2,1)}, u32[]{:S(2)}) %copy-start) | copy-done | bytes 2359320
  2.3 1.2 %pack.1 = (bf16[3,2,3,3,80,128]{5,4,3,2,1,0:T(8,128)(2,1)S(1)}, bf16[3,2,3,3,48,128]{5,4,3,2,1,0:T(8,128)(2,1)}, bf16[1,2,3,3,128,128]{5,4,3,2,1,0:T(8,128)(2,1)S(1)}) custom-call(bf16[4,2,3,3,128,128]{5,4,3,2,1,0:T(8,128)(2,1)S(1)} %copy-done), custom_call_target="tpu_custom_call" | custom-call | flops 1000 | bytes 1000 | tf_op jit(solution)/shard_map/pack/pallas_call | solution.py:570
  3.5 5.5 %collective-permute-start.2 = (bf16[3,2,3,3,80,128]{5,4,3,2,1,0:T(8,128)(2,1)S(1)}, bf16[3,2,3,3,80,128]{5,4,3,2,1,0:T(8,128)(2,1)S(1)}, u32[]{:S(2)}, u32[]{:S(2)}) collective-permute-start(bf16[3,2,3,3,80,128]{5,4,3,2,1,0:T(8,128)(2,1)S(1)} %get-tuple-element.13.level), channel_id=1, source_target_pairs={{1,0},{2,1},{3,2},{4,3},{5,4},{6,5},{7,6},{8,7},{9,8},{10,9},{11,1... | collective-permute-start | bytes 3317768 | tf_op jit(solution)/shard_map/ppermute | solution.py:31
  8.9 1.8 %staples.3 = bf16[5,54,16,128]{3,2,1,0:T(8,128)(2,1)S(1)} custom-call(bf16[3,2,3,3,80,128]{5,4,3,2,1,0:T(8,128)(2,1)S(1)} %get-tuple-element.13.level, bf16[1,2,3,3,128,128]{5,4,3,2,1,0:T(8,128)(2,1)S(1)} %get-tuple-element.12.upward), custom_call_target="tpu_custom_call" | custom-call | flops 1000 | bytes 1000 | tf_op jit(solution)/shard_map/staples/pallas_call | solution.py:586
  10.8 0.0 copy-start.1
  10.8 0.1 collective-permute-start.3
  10.8 4.4 %collective-permute-start = (bf16[3,2,3,3,48,128]{5,4,3,2,1,0:T(8,128)(2,1)}, bf16[3,2,3,3,48,128]{5,4,3,2,1,0:T(8,128)(2,1)}, u32[]{:S(2)}, u32[]{:S(2)}) collective-permute-start(bf16[3,2,3,3,48,128]{5,4,3,2,1,0:T(8,128)(2,1)} %get-tuple-element.11.level), channel_id=1, source_target_pairs={{1,0},{2,1},{3,2},{4,3},{5,4},{6,5},{7,6},{8,7},{9,8},{10,9},{11,1... | collective-permute-start | bytes 1990664 | tf_op jit(solution)/shard_map/ppermute | solution.py:31
  15.3 3.1 %staples.2 = bf16[3,54,16,128]{3,2,1,0:T(8,128)(2,1)} custom-call(bf16[3,2,3,3,48,128]{5,4,3,2,1,0:T(8,128)(2,1)} %get-tuple-element.11.level, bf16[1,2,3,3,128,128]{5,4,3,2,1,0:T(8,128)(2,1)S(1)} %get-tuple-element.12.upward), custom_call_target="tpu_custom_call" | custom-call | flops 1000 | bytes 1000 | tf_op jit(solution)/shard_map/staples/pallas_call | solution.py:586
  18.3 0.0 collective-permute-start.1
  18.3 0.0 copy-done.1
  18.3 1.9 %spread.1 = bf16[16,384,128]{2,1,0:T(8,128)(2,1)} custom-call(bf16[48,8,2048]{2,1,0:T(8,128)(2,1)S(1)} %bitcast.6), custom_call_target="tpu_custom_call" | custom-call | flops 1000 | bytes 1000 | tf_op jit(solution)/shard_map/spread/pallas_call | solution.py:600
  20.2 0.0 copy-start.2
  20.2 0.0 copy-start.6
  20.2 0.0 copy-start.7
  20.2 0.0 copy-start.8
  20.2 6.0 %all-to-all-start = ((bf16[16,384,128]{2,1,0:T(8,128)(2,1)}), bf16[16,384,128]{2,1,0:T(8,128)(2,1)}, u32[]{:S(2)}, u32[]{:S(2)}) async-start(bf16[16,384,128]{2,1,0:T(8,128)(2,1)} %spread.1), calls=%async_computation | async-start | bytes 3145728 | tf_op jit(solution)/shard_map/all_to_all | solution.py:616
  26.2 0.0 copy-done.2
  26.3 0.2 slice_reduce_fusion.2
  26.4 0.0 copy-done.6
  26.5 0.0 copy-done.7
  26.5 0.0 copy-done.8
  26.5 0.1 fusion.20
  26.6 0.0 copy-start.5
  26.6 0.0 copy-start.3
  26.6 0.0 copy-start.10
  26.6 0.0 copy-start.4
  26.6 12.1 %flat_planes.1.refs_4_ = f32[8,27,16,128]{3,2,1,0:T(8,128)} custom-call(bf16[4,2,3,3,128,128]{5,4,3,2,1,0:T(8,128)(2,1)} %refs_1_.3), custom_call_target="tpu_custom_call" | custom-call | flops 1000 | bytes 1000 | tf_op jit(solution)/shard_map/flat_planes/pallas_call | solution.py:626
  38.8 0.0 copy-done.5
  38.8 0.2 convert_reduce_fusion
  39.0 0.0 copy-done.3
  39.0 0.0 copy-done.10
  39.0 0.1 fusion.16
  39.1 0.0 copy-done.4
  39.1 0.6 broadcast_bitcast_fusion.turn
  39.7 0.8 fusion.owner
  40.5 0.0 collective-permute-done.3.refs_3_
  40.5 0.0 collective-permute-done.2.refs_2_
  40.5 0.0 copy-start.9
  40.5 1.0 %copy-done.9 = bf16[3,2,3,3,80,128]{5,4,3,2,1,0:T(8,128)(2,1)} copy-done((bf16[3,2,3,3,80,128]{5,4,3,2,1,0:T(8,128)(2,1)}, bf16[3,2,3,3,80,128]{5,4,3,2,1,0:T(8,128)(2,1)S(1)}, u32[]{:S(2)}) %copy-start.9) | copy-done | bytes 1105944
  41.6 8.3 %insertion.2 = (bf16[2,2,4,3,128,128]{5,4,3,2,1,0:T(8,128)(2,1)}, f32[8,48,16,128]{3,2,1,0:T(8,128)}, f32[9,16,128]{2,1,0:T(8,128)}, f32[27,16,128]{2,1,0:T(8,128)}) custom-call(bf16[4,2,3,3,128,128]{5,4,3,2,1,0:T(8,128)(2,1)} %refs_1_.3, bf16[4,2,3,3,128,128]{5,4,3,2,1,0:T(8,128)(2,1)} %refs_1_.3, bf16[3,2,3,3,80,128]{5,4,3,2,1,0:T(8,128)(2,1)} %copy-done.9, ...), custom_call_target="tpu_custom_call" | custom-call | flops 999999995904 | bytes 1000 | tf_op jit(solution)/shard_map/insertion/pallas_call | solution.py:688
  49.9 0.0 collective-permute-done.1.refs_3_
  49.9 0.0 collective-permute-done.refs_2_
  49.9 6.9 %insertion.3 = (bf16[2,2,4,3,128,128]{5,4,3,2,1,0:T(8,128)(2,1)}, f32[8,48,16,128]{3,2,1,0:T(8,128)}) custom-call(bf16[4,2,3,3,128,128]{5,4,3,2,1,0:T(8,128)(2,1)} %refs_1_.3, bf16[4,2,3,3,128,128]{5,4,3,2,1,0:T(8,128)(2,1)} %refs_1_.3, bf16[3,2,3,3,48,128]{5,4,3,2,1,0:T(8,128)(2,1)} %collective-permute-done.refs_2_, ...), custom_call_target="tpu_custom_call", output_to_operand_aliasing={{0}: (8, {}), {1}: (9, {})} | custom-call | flops 999999995904 | bytes 1000 | tf_op jit(solution)/shard_map/insertion/pallas_call | solution.py:688
  56.8 6.3 %all-to-all-done.sink = bf16[16,384,128]{2,1,0:T(8,128)(2,1)} async-done(((bf16[16,384,128]{2,1,0:T(8,128)(2,1)}), bf16[16,384,128]{2,1,0:T(8,128)(2,1)}, u32[]{:S(2)}, u32[]{:S(2)}) %all-to-all-start) | async-done | bytes 1572896 | tf_op jit(solution)/shard_map/all_to_all | solution.py:616
  63.1 4.2 %projection.1 = f32[128,256]{1,0:T(8,128)} custom-call(f32[8,48,16,128]{3,2,1,0:T(8,128)} %get-tuple-element.19.crossed, bf16[16,384,128]{2,1,0:T(8,128)(2,1)} %all-to-all-done.sink, bf16[2,128,256]{2,1,0:T(8,128)(2,1)} %constant.77.clone.wave_y, f32[2,16,128]{2,1,0:T(8,128)} %constant.78.clone.wave_x, f32[2,16,128]{2,1,0:T(8,128)} %broadcast_bitcast_fusion.turn, ...), custom_call_target="tpu_custom_call" | custom-call | flops 1000 | bytes 1000 | tf_op jit(solution)/shard_map/projection/pallas_call | solution.py:716
  67.3 18.3 %all_to_all.10 = f32[16,8,256]{2,1,0:T(8,128)S(1)} all-to-all(f32[16,8,256]{2,1,0:T(8,128)} %bitcast.7), channel_id=1, replica_groups=mesh['grp'=2,'space'=16] {'space'}, dimensions={0} | all-to-all | bytes 262144 | tf_op jit(solution)/shard_map/all_to_all | solution.py:731
  85.5 0.6 slice_reduce_fusion
  (2 shorter events, 0.0 us)
Async XLA Ops:
  0.6 1.7 %copy-start = (bf16[4,2,3,3,128,128]{5,4,3,2,1,0:T(8,128)(2,1)S(1)}, bf16[4,2,3,3,128,128]{5,4,3,2,1,0:T(8,128)(2,1)}, u32[]{:S(2)}) copy-start(bf16[4,2,3,3,128,128]{5,4,3,2,1,0:T(8,128)(2,1)} %refs_1_.3) | copy-start | bytes 7077892
  3.5 37.0 %collective-permute-start.2 = (bf16[3,2,3,3,80,128]{5,4,3,2,1,0:T(8,128)(2,1)S(1)}, bf16[3,2,3,3,80,128]{5,4,3,2,1,0:T(8,128)(2,1)S(1)}, u32[]{:S(2)}, u32[]{:S(2)}) collective-permute-start(bf16[3,2,3,3,80,128]{5,4,3,2,1,0:T(8,128)(2,1)S(1)} %get-tuple-element.13.level), channel_id=1, source_target_pairs={{1,0},{2,1},{3,2},{4,3},{5,4},{6,5},{7,6},{8,7},{9,8},{10,9},{11,1... | collective-permute-start | bytes 3317768 | tf_op jit(solution)/shard_map/ppermute | solution.py:31
  10.8 7.6 %copy-start.1 = (bf16[2,2,4,3,8,2048]{5,4,3,2,1,0:T(8,128)(2,1)S(1)}, bf16[2,2,4,3,8,2048]{5,4,3,2,1,0:T(8,128)(2,1)}, u32[]{:S(2)}) copy-start(bf16[2,2,4,3,8,2048]{5,4,3,2,1,0:T(8,128)(2,1)} %param.15) | copy-start | bytes 4718596
  10.8 29.7 %collective-permute-start.3 = (bf16[5,54,16,128]{3,2,1,0:T(8,128)(2,1)S(1)}, bf16[5,54,16,128]{3,2,1,0:T(8,128)(2,1)}, u32[]{:S(2)}, u32[]{:S(2)}) collective-permute-start(bf16[5,54,16,128]{3,2,1,0:T(8,128)(2,1)S(1)} %staples.3), channel_id=1, source_target_pairs={{15,0},{0,1},{1,2},{2,3},{3,4},{4,5},{5,6},{6,7},{7,8},{8,9},{9,10... | collective-permute-start | bytes 3317768 | tf_op jit(solution)/shard_map/ppermute | solution.py:31
  10.8 39.1 %collective-permute-start = (bf16[3,2,3,3,48,128]{5,4,3,2,1,0:T(8,128)(2,1)}, bf16[3,2,3,3,48,128]{5,4,3,2,1,0:T(8,128)(2,1)}, u32[]{:S(2)}, u32[]{:S(2)}) collective-permute-start(bf16[3,2,3,3,48,128]{5,4,3,2,1,0:T(8,128)(2,1)} %get-tuple-element.11.level), channel_id=1, source_target_pairs={{1,0},{2,1},{3,2},{4,3},{5,4},{6,5},{7,6},{8,7},{9,8},{10,9},{11,1... | collective-permute-start | bytes 1990664 | tf_op jit(solution)/shard_map/ppermute | solution.py:31
  18.3 31.6 %collective-permute-start.1 = (bf16[3,54,16,128]{3,2,1,0:T(8,128)(2,1)}, bf16[3,54,16,128]{3,2,1,0:T(8,128)(2,1)}, u32[]{:S(2)}, u32[]{:S(2)}) collective-permute-start(bf16[3,54,16,128]{3,2,1,0:T(8,128)(2,1)} %staples.2), channel_id=1, source_target_pairs={{15,0},{0,1},{1,2},{2,3},{3,4},{4,5},{5,6},{6,7},{7,8},{8,9},{9,10... | collective-permute-start | bytes 1990664 | tf_op jit(solution)/shard_map/ppermute | solution.py:31
  20.2 6.0 %copy-start.2 = (s32[2,3]{1,0:T(2,128)S(1)}, s32[2,3]{1,0:T(2,128)}, u32[]{:S(2)}) copy-start(s32[2,3]{1,0:T(2,128)} %param.17) | copy-start | bytes 76
  20.2 6.2 %copy-start.6 = (s32[128]{0:T(128)S(1)}, s32[128]{0:T(128)}, u32[]{:S(2)}) copy-start(s32[128]{0:T(128)} %constant.74.clone) | copy-start | bytes 1540
  20.2 6.2 %copy-start.7 = (s32[128]{0:T(128)S(1)}, s32[128]{0:T(128)}, u32[]{:S(2)}) copy-start(s32[128]{0:T(128)} %constant.75.clone) | copy-start | bytes 1540
  20.2 6.2 %copy-start.8 = (s32[128]{0:T(128)S(1)}, s32[128]{0:T(128)}, u32[]{:S(2)}) copy-start(s32[128]{0:T(128)} %constant.76.clone) | copy-start | bytes 1540
  20.2 42.9 %all-to-all-start = ((bf16[16,384,128]{2,1,0:T(8,128)(2,1)}), bf16[16,384,128]{2,1,0:T(8,128)(2,1)}, u32[]{:S(2)}, u32[]{:S(2)}) async-start(bf16[16,384,128]{2,1,0:T(8,128)(2,1)} %spread.1), calls=%async_computation | async-start | bytes 3145728 | tf_op jit(solution)/shard_map/all_to_all | solution.py:616
  26.6 12.2 %copy-start.5 = (s32[32,1]{0,1:T(1,128)S(1)}, s32[32,1]{0,1:T(1,128)}, u32[]{:S(2)}) copy-start(s32[32,1]{0,1:T(1,128)} %param.20) | copy-start | bytes 388
  26.6 12.4 %copy-start.3 = (s32[32]{0:T(128)S(1)}, s32[32]{0:T(128)}, u32[]{:S(2)}) copy-start(s32[32]{0:T(128)} %param.18) | copy-start | bytes 388
  26.6 12.3 %copy-start.10 = (s32[2]{0:T(128)S(1)}, s32[2]{0:T(128)}, u32[]{:S(2)}) copy-start(s32[2]{0:T(128)} %param.16) | copy-start | bytes 28
  26.6 12.4 %copy-start.4 = (s32[32]{0:T(128)S(1)}, s32[32]{0:T(128)}, u32[]{:S(2)}) copy-start(s32[32]{0:T(128)} %param.19) | copy-start | bytes 388
  40.5 1.1 %copy-start.9 = (bf16[3,2,3,3,80,128]{5,4,3,2,1,0:T(8,128)(2,1)}, bf16[3,2,3,3,80,128]{5,4,3,2,1,0:T(8,128)(2,1)S(1)}, u32[]{:S(2)}) copy-start(bf16[3,2,3,3,80,128]{5,4,3,2,1,0:T(8,128)(2,1)S(1)} %collective-permute-done.2.refs_2_) | copy-start | bytes 3317764

commit v3 on v2

--- a/solution.py
+++ b/solution.py
@@ -454,9 +454,11 @@
     turned = jnp.concatenate(
         [sum_re * cos_t - sum_im * sin_t, sum_re * sin_t + sum_im * cos_t], axis=1
     )
-    out[...] = jnp.dot(
-        owner[...], turned, precision=lax.Precision.HIGHEST, preferred_element_type=F32
-    )
+    parts = []
+    for _ in range(3):
+        parts.append(turned.astype(BF16))
+        turned = turned - parts[-1].astype(F32)
+    out[...] = both(owner[...], jnp.concatenate(parts, axis=0))
 
 
 def pack_kernel(links, *refs):
@@ -546,7 +548,8 @@
     earlier = (owner[:, None] == owner[None, :]) & (number[None, :] < number[:, None])
     target = owner * PADDED + jnp.sum(earlier.astype(jnp.int32), axis=1)
     rows = jnp.arange(row_count, dtype=jnp.int32)[:, None] == target[None, :]
-    return jnp.dot(rows.astype(BF16), picks.astype(BF16), preferred_element_type=F32)
+    table = jnp.dot(rows.astype(BF16), picks.astype(BF16), preferred_element_type=F32)
+    return jnp.concatenate([table.astype(BF16)] * 3, axis=1)
 
 
 def on_device(
@@ -577,7 +580,7 @@
         in_specs=[pl.BlockSpec(memory_space=pl.ANY)],
         out_specs=whole(len(PIECES) + 1),
         scratch_shapes=[pltpu.SemaphoreType.DMA((2 * len(PIECES) + 1,))],
-        compiler_params=params(6),
+        compiler_params=params(50),
         cost_estimate=cost(1000, 1000),
         name="pack",
     )(gauge_links)
@@ -698,7 +701,7 @@
                 pltpu.VMEM((2, HALF + 18, LX, LY), F32),
             ],
             compiler_params=params(),
-            cost_estimate=cost(10**12, 1000),
+            cost_estimate=cost(8 * 10**10 if first else 1000, 1000),
             name="insertion",
         )(*operands)
         inserted, crossed = results[:2]

time: 86.7 us -> 85.2 us (0.983)
  local copies, waits for them, and re-layouts: 3.36 us -> 1.36 us
  Pallas kernels: 39.4 us -> 37.7 us
  waiting for transfers between devices: 6.33 us -> 7.88 us
  other arithmetic: 1.2 us -> 2.4 us
    unnamed x22 -> x14, local copies, waits for them, and re-layouts: 2.76 us -> 0.03 us
    pallas_call x2, Pallas kernels: 4.88 us -> 2.92 us  [piece_staples(): pl.pallas_call(functools.partial(staple_kernel, begin), out_shape=jax.Sha...]
    all_to_all x1, waiting for transfers between devices: 6.32 us -> 7.87 us  [on_device(): lax.all_to_all(spread, 'space', split_axis=0, concat_axis=0, tiled=True)]
  transfers between devices with their start and end apart: 5 -> 5, of which waited for: 1 -> 1; matrix products, arithmetic and copies ran while one was open for 2% -> 4% of each run, Pallas kernels for 40% -> 38%
where the time goes in v3:
time: 85.2 us; the launch traced here: 84.7 us
  Pallas kernels  37.7 us (44%)
  blocking collectives  18.4 us (22%)
  starting transfers between devices  16 us (19%)
  waiting for transfers between devices  7.88 us (9%)
  other arithmetic  2.4 us (3%)
  local copies, waits for them, and re-layouts  1.36 us (2%)
    all_to_all x1, blocking collectives, on_device(): lax.all_to_all(rows.reshape(devices, PADDED, 2 * NMOM), 'space', split_ax...  18.4 us
    pallas_call x2, Pallas kernels, on_device(): pl.pallas_call(functools.partial(insert_kernel, begin, end), grid=(end -...  15.3 us
    pallas_call x1, Pallas kernels, on_device(): pl.pallas_call(flat_kernel, out_shape=jax.ShapeDtypeStruct((LT, 3 * HALF,...  12.1 us
    ppermute x4, starting transfers between devices, from_behind(): lax.ppermute(block, 'space', [((i - distance) % count, i) for i in range(...  10 us
    all_to_all x1, waiting for transfers between devices, on_device(): lax.all_to_all(spread, 'space', split_axis=0, concat_axis=0, tiled=True)  7.87 us
    all_to_all x1, starting transfers between devices, on_device(): lax.all_to_all(spread, 'space', split_axis=0, concat_axis=0, tiled=True)  5.98 us
    pallas_call x1, Pallas kernels, on_device(): pl.pallas_call(functools.partial(project_kernel, sources), grid=(steps,),...  3.91 us
    pallas_call x2, Pallas kernels, piece_staples(): pl.pallas_call(functools.partial(staple_kernel, begin), out_shape=jax.Sha...  2.92 us
  transfers between devices with their start and end apart: 5, of which 1 were waited for; matrix products, arithmetic and copies ran while one was open for 4% of the time, Pallas kernels for 38%

profile of v3, /device:TPU:0, one launch (start us, length us, event | category | flops | bytes accessed | tf_op | source)
XLA Modules:
  0.0 84.7 jit_solution(7483178250200375883)
XLA Ops:
  0.6 1.6 %pack.1 = (bf16[3,2,3,3,80,128]{5,4,3,2,1,0:T(8,128)(2,1)S(1)}, bf16[3,2,3,3,48,128]{5,4,3,2,1,0:T(8,128)(2,1)S(1)}, bf16[1,2,3,3,128,128]{5,4,3,2,1,0:T(8,128)(2,1)S(1)}) custom-call(bf16[4,2,3,3,128,128]{5,4,3,2,1,0:T(8,128)(2,1)} %refs_1_.3), custom_call_target="tpu_custom_call" | custom-call | flops 1000 | bytes 1000 | tf_op jit(solution)/shard_map/pack/pallas_call | solution.py:573
  2.3 5.5 %collective-permute-start.2 = (bf16[3,2,3,3,80,128]{5,4,3,2,1,0:T(8,128)(2,1)S(1)}, bf16[3,2,3,3,80,128]{5,4,3,2,1,0:T(8,128)(2,1)}, u32[]{:S(2)}, u32[]{:S(2)}) collective-permute-start(bf16[3,2,3,3,80,128]{5,4,3,2,1,0:T(8,128)(2,1)S(1)} %get-tuple-element.13.level), channel_id=1, source_target_pairs={{1,0},{2,1},{3,2},{4,3},{5,4},{6,5},{7,6},{8,7},{9,8},{10,9},{11,1... | collective-permute-start | bytes 3317768 | tf_op jit(solution)/shard_map/ppermute | solution.py:31
  7.8 1.8 %staples.3 = bf16[5,54,16,128]{3,2,1,0:T(8,128)(2,1)S(1)} custom-call(bf16[3,2,3,3,80,128]{5,4,3,2,1,0:T(8,128)(2,1)S(1)} %get-tuple-element.13.level, bf16[1,2,3,3,128,128]{5,4,3,2,1,0:T(8,128)(2,1)S(1)} %get-tuple-element.12.upward), custom_call_target="tpu_custom_call" | custom-call | flops 1000 | bytes 1000 | tf_op jit(solution)/shard_map/staples/pallas_call | solution.py:589
  9.6 0.0 copy-start
  9.6 0.1 collective-permute-start.3
  9.7 4.4 %collective-permute-start = (bf16[3,2,3,3,48,128]{5,4,3,2,1,0:T(8,128)(2,1)S(1)}, bf16[3,2,3,3,48,128]{5,4,3,2,1,0:T(8,128)(2,1)}, u32[]{:S(2)}, u32[]{:S(2)}) collective-permute-start(bf16[3,2,3,3,48,128]{5,4,3,2,1,0:T(8,128)(2,1)S(1)} %get-tuple-element.11.level), channel_id=1, source_target_pairs={{1,0},{2,1},{3,2},{4,3},{5,4},{6,5},{7,6},{8,7},{9,8},{10,9},{11,1... | collective-permute-start | bytes 1990664 | tf_op jit(solution)/shard_map/ppermute | solution.py:31
  14.1 1.1 %staples.2 = bf16[3,54,16,128]{3,2,1,0:T(8,128)(2,1)S(1)} custom-call(bf16[3,2,3,3,48,128]{5,4,3,2,1,0:T(8,128)(2,1)S(1)} %get-tuple-element.11.level, bf16[1,2,3,3,128,128]{5,4,3,2,1,0:T(8,128)(2,1)S(1)} %get-tuple-element.12.upward), custom_call_target="tpu_custom_call" | custom-call | flops 1000 | bytes 1000 | tf_op jit(solution)/shard_map/staples/pallas_call | solution.py:589
  15.2 0.1 collective-permute-start.1
  15.3 0.0 copy-done
  15.3 1.9 %spread.1 = bf16[16,384,128]{2,1,0:T(8,128)(2,1)} custom-call(bf16[48,8,2048]{2,1,0:T(8,128)(2,1)S(1)} %bitcast.6), custom_call_target="tpu_custom_call" | custom-call | flops 1000 | bytes 1000 | tf_op jit(solution)/shard_map/spread/pallas_call | solution.py:603
  17.2 0.0 copy-start.4
  17.2 0.0 copy-start.2
  17.2 0.0 copy-start.6
  17.2 0.0 copy-start.3
  17.2 6.0 %all-to-all-start = ((bf16[16,384,128]{2,1,0:T(8,128)(2,1)}), bf16[16,384,128]{2,1,0:T(8,128)(2,1)}, u32[]{:S(2)}, u32[]{:S(2)}) async-start(bf16[16,384,128]{2,1,0:T(8,128)(2,1)} %spread.1), calls=%async_computation | async-start | bytes 3145728 | tf_op jit(solution)/shard_map/all_to_all | solution.py:619
  23.2 0.0 copy-done.4
  23.2 0.2 convert_reduce_fusion
  23.4 0.0 copy-done.2
  23.4 0.0 copy-done.6
  23.4 0.1 fusion.15
  23.5 0.0 copy-done.3
  23.5 0.5 fusion.16
  24.0 0.0 copy-start.5
  24.0 0.0 copy-start.1
  24.0 12.1 %flat_planes.1.refs_4_ = f32[8,27,16,128]{3,2,1,0:T(8,128)} custom-call(bf16[4,2,3,3,128,128]{5,4,3,2,1,0:T(8,128)(2,1)} %refs_1_.3), custom_call_target="tpu_custom_call" | custom-call | flops 1000 | bytes 1000 | tf_op jit(solution)/shard_map/flat_planes/pallas_call | solution.py:629
  36.1 0.0 copy-done.5
  36.1 0.2 convolution_convert_fusion
  36.3 0.7 copy.19.owner
  37.0 0.0 copy-done.1
  37.1 0.2 slice_reduce_fusion.2
  37.2 0.8 fusion.19
  38.1 0.6 broadcast_bitcast_fusion.turn
  38.7 0.0 collective-permute-done.3.refs_3_
  38.7 0.0 collective-permute-done.2.refs_2_
  38.7 8.4 %insertion.2 = (bf16[2,2,4,3,128,128]{5,4,3,2,1,0:T(8,128)(2,1)}, f32[8,48,16,128]{3,2,1,0:T(8,128)}, f32[9,16,128]{2,1,0:T(8,128)}, f32[27,16,128]{2,1,0:T(8,128)}) custom-call(bf16[4,2,3,3,128,128]{5,4,3,2,1,0:T(8,128)(2,1)} %refs_1_.3, bf16[4,2,3,3,128,128]{5,4,3,2,1,0:T(8,128)(2,1)} %refs_1_.3, ...), custom_call_target="tpu_custom_call" | custom-call | flops 80000000000 | bytes 1000 | tf_op jit(solution)/shard_map/insertion/pallas_call | solution.py:691
  47.1 0.0 collective-permute-done.1.refs_3_
  47.1 0.0 collective-permute-done.refs_2_
  47.1 6.9 %insertion.3 = (bf16[2,2,4,3,128,128]{5,4,3,2,1,0:T(8,128)(2,1)}, f32[8,48,16,128]{3,2,1,0:T(8,128)}) custom-call(bf16[4,2,3,3,128,128]{5,4,3,2,1,0:T(8,128)(2,1)} %refs_1_.3, bf16[4,2,3,3,128,128]{5,4,3,2,1,0:T(8,128)(2,1)} %refs_1_.3, bf16[3,2,3,3,48,128]{5,4,3,2,1,0:T(8,128)(2,1)} %collective-permute-done.refs_2_, ...), custom_call_target="tpu_custom_call", output_to_operand_aliasing={{0}: (8, {}), {1}: (9, {})} | custom-call | flops 1000 | bytes 1000 | tf_op jit(solution)/shard_map/insertion/pallas_call | solution.py:691
  53.9 7.9 %all-to-all-done.sink = bf16[16,384,128]{2,1,0:T(8,128)(2,1)} async-done(((bf16[16,384,128]{2,1,0:T(8,128)(2,1)}), bf16[16,384,128]{2,1,0:T(8,128)(2,1)}, u32[]{:S(2)}, u32[]{:S(2)}) %all-to-all-start) | async-done | bytes 1572896 | tf_op jit(solution)/shard_map/all_to_all | solution.py:619
  61.8 3.9 %projection.1 = f32[128,256]{1,0:T(8,128)} custom-call(f32[8,48,16,128]{3,2,1,0:T(8,128)} %get-tuple-element.19.crossed, bf16[16,384,128]{2,1,0:T(8,128)(2,1)} %all-to-all-done.sink, bf16[2,128,256]{2,1,0:T(8,128)(2,1)} %constant.77.clone.wave_y, f32[2,16,128]{2,1,0:T(8,128)} %constant.78.clone.wave_x, f32[2,16,128]{2,1,0:T(8,128)} %broadcast_bitcast_fusion.turn, ...), custom_call_target="tpu_custom_call" | custom-call | flops 1000 | bytes 1000 | tf_op jit(solution)/shard_map/projection/pallas_call | solution.py:719
  65.7 18.4 %all_to_all.10 = f32[16,8,256]{2,1,0:T(8,128)S(1)} all-to-all(f32[16,8,256]{2,1,0:T(8,128)} %bitcast.7), channel_id=1, replica_groups=mesh['grp'=2,'space'=16] {'space'}, dimensions={0} | all-to-all | bytes 262144 | tf_op jit(solution)/shard_map/all_to_all | solution.py:734
  84.1 0.6 slice_reduce_fusion
  (2 shorter events, 0.0 us)
Async XLA Ops:
  2.3 36.4 %collective-permute-start.2 = (bf16[3,2,3,3,80,128]{5,4,3,2,1,0:T(8,128)(2,1)S(1)}, bf16[3,2,3,3,80,128]{5,4,3,2,1,0:T(8,128)(2,1)}, u32[]{:S(2)}, u32[]{:S(2)}) collective-permute-start(bf16[3,2,3,3,80,128]{5,4,3,2,1,0:T(8,128)(2,1)S(1)} %get-tuple-element.13.level), channel_id=1, source_target_pairs={{1,0},{2,1},{3,2},{4,3},{5,4},{6,5},{7,6},{8,7},{9,8},{10,9},{11,1... | collective-permute-start | bytes 3317768 | tf_op jit(solution)/shard_map/ppermute | solution.py:31
  9.6 5.7 %copy-start = (bf16[2,2,4,3,8,2048]{5,4,3,2,1,0:T(8,128)(2,1)S(1)}, bf16[2,2,4,3,8,2048]{5,4,3,2,1,0:T(8,128)(2,1)}, u32[]{:S(2)}) copy-start(bf16[2,2,4,3,8,2048]{5,4,3,2,1,0:T(8,128)(2,1)} %param.15) | copy-start | bytes 4718596
  9.6 29.1 %collective-permute-start.3 = (bf16[5,54,16,128]{3,2,1,0:T(8,128)(2,1)S(1)}, bf16[5,54,16,128]{3,2,1,0:T(8,128)(2,1)}, u32[]{:S(2)}, u32[]{:S(2)}) collective-permute-start(bf16[5,54,16,128]{3,2,1,0:T(8,128)(2,1)S(1)} %staples.3), channel_id=1, source_target_pairs={{15,0},{0,1},{1,2},{2,3},{3,4},{4,5},{5,6},{6,7},{7,8},{8,9},{9,10... | collective-permute-start | bytes 3317768 | tf_op jit(solution)/shard_map/ppermute | solution.py:31
  9.7 37.4 %collective-permute-start = (bf16[3,2,3,3,48,128]{5,4,3,2,1,0:T(8,128)(2,1)S(1)}, bf16[3,2,3,3,48,128]{5,4,3,2,1,0:T(8,128)(2,1)}, u32[]{:S(2)}, u32[]{:S(2)}) collective-permute-start(bf16[3,2,3,3,48,128]{5,4,3,2,1,0:T(8,128)(2,1)S(1)} %get-tuple-element.11.level), channel_id=1, source_target_pairs={{1,0},{2,1},{3,2},{4,3},{5,4},{6,5},{7,6},{8,7},{9,8},{10,9},{11,1... | collective-permute-start | bytes 1990664 | tf_op jit(solution)/shard_map/ppermute | solution.py:31
  15.2 31.9 %collective-permute-start.1 = (bf16[3,54,16,128]{3,2,1,0:T(8,128)(2,1)S(1)}, bf16[3,54,16,128]{3,2,1,0:T(8,128)(2,1)}, u32[]{:S(2)}, u32[]{:S(2)}) collective-permute-start(bf16[3,54,16,128]{3,2,1,0:T(8,128)(2,1)S(1)} %staples.2), channel_id=1, source_target_pairs={{15,0},{0,1},{1,2},{2,3},{3,4},{4,5},{5,6},{6,7},{7,8},{8,9},{9,10... | collective-permute-start | bytes 1990664 | tf_op jit(solution)/shard_map/ppermute | solution.py:31
  17.2 6.0 %copy-start.4 = (s32[32,1]{0,1:T(1,128)S(1)}, s32[32,1]{0,1:T(1,128)}, u32[]{:S(2)}) copy-start(s32[32,1]{0,1:T(1,128)} %param.20) | copy-start | bytes 388
  17.2 6.2 %copy-start.2 = (s32[32]{0:T(128)S(1)}, s32[32]{0:T(128)}, u32[]{:S(2)}) copy-start(s32[32]{0:T(128)} %param.18) | copy-start | bytes 388
  17.2 6.2 %copy-start.6 = (s32[2]{0:T(128)S(1)}, s32[2]{0:T(128)}, u32[]{:S(2)}) copy-start(s32[2]{0:T(128)} %param.16) | copy-start | bytes 28
  17.2 6.3 %copy-start.3 = (s32[32]{0:T(128)S(1)}, s32[32]{0:T(128)}, u32[]{:S(2)}) copy-start(s32[32]{0:T(128)} %param.19) | copy-start | bytes 388
  17.2 44.6 %all-to-all-start = ((bf16[16,384,128]{2,1,0:T(8,128)(2,1)}), bf16[16,384,128]{2,1,0:T(8,128)(2,1)}, u32[]{:S(2)}, u32[]{:S(2)}) async-start(bf16[16,384,128]{2,1,0:T(8,128)(2,1)} %spread.1), calls=%async_computation | async-start | bytes 3145728 | tf_op jit(solution)/shard_map/all_to_all | solution.py:619
  24.0 12.1 %copy-start.5 = (s32[32]{0:T(128)S(1)}, s32[32]{0:T(128)}, u32[]{:S(2)}) copy-start(s32[32]{0:T(128)} %get-tuple-element.26) | copy-start | bytes 388
  24.0 13.0 %copy-start.1 = (s32[2,3]{1,0:T(2,128)S(1)}, s32[2,3]{1,0:T(2,128)}, u32[]{:S(2)}) copy-start(s32[2,3]{1,0:T(2,128)} %param.17) | copy-start | bytes 76

commit v4 on v3

--- a/solution.py
+++ b/solution.py
@@ -22,7 +22,7 @@
 PADDED = 8
 UPPER = ((0, 1), (0, 2), (1, 2))
 SYMMETRIC = ((0, 0), (1, 1), (2, 2), (0, 1), (0, 2), (1, 2))
-HALVES = (slice(0, 8), slice(8, 16))
+HALVES = (slice(0, 16),)
 HALF = len(UPPER) + len(SYMMETRIC)
 
 
@@ -269,16 +269,18 @@
     for block in range(2):
         for source in range(plain.shape[0]):
             rounded = {}
+            whole_spinor = [
+                [
+                    tuple(
+                        plain[source, part, 2 * block + spin, color].astype(F32) for part in (0, 1)
+                    )
+                    for color in range(3)
+                ]
+                for spin in range(2)
+            ]
             for half in HALVES:
                 spinor = [
-                    [
-                        tuple(
-                            plain[source, part, 2 * block + spin, color].astype(F32)[half]
-                            for part in (0, 1)
-                        )
-                        for color in range(3)
-                    ]
-                    for spin in range(2)
+                    [tuple(part[half] for part in item) for item in row] for row in whole_spinor
                 ]
                 for spin in range(2):
                     for i in range(3):
@@ -329,10 +331,7 @@
                         inserted[source, part, 2 * block + spin, i] = value
                         kept.append(value.astype(F32))
                     result.append(kept)
-                vector = [
-                    [plain[source, part, 2 * block + spin, color].astype(F32) for part in (0, 1)]
-                    for color in range(3)
-                ]
+                vector = whole_spinor[spin]
                 for a, b, c in ((0, 1, 2), (1, 2, 0), (2, 0, 1)):
                     (a_re, a_im), (b_re, b_im) = result[a], result[b]
                     (p_re, p_im), (q_re, q_im) = vector[a], vector[b]
@@ -644,13 +643,13 @@
         first, last = begin == 0, end == LT
 
         def now(step):
-            return lax.rem(begin + step, LT)
+            return begin + own(step)
 
         def own(step):
             return jnp.minimum(step, end - begin - 1)
 
         def later(step):
-            return lax.rem(begin + step + 1, LT)
+            return lax.rem(begin + own(step) + 1, LT)
 
         def written(step):
             return lax.rem(begin + (jnp.maximum(step, 1) if first else step), LT)
@@ -661,8 +660,8 @@
             up_block(later),
             slab_block(matrices, own),
             pl.BlockSpec((1, 54, LX, LY), lambda step: (own(step), 0, 0, 0)),
-            pl.BlockSpec((1, 3 * HALF, LX, LY), lambda step: (now(step), 0, 0, 0)),
-            slab_block(spinors, now),
+            pl.BlockSpec((1, 3 * HALF, LX, LY), lambda step: (written(step), 0, 0, 0)),
+            slab_block(spinors, written),
         ]
         shapes = [
             jax.ShapeDtypeStruct(propagators.shape, BF16),

time: 85.2 us -> 85.2 us (level)
  no operation moved by 1% of the time
where the time goes in v4:
time: 85.2 us; the launch traced here: 84.7 us
  Pallas kernels  37.6 us (44%)
  blocking collectives  18.3 us (21%)
  starting transfers between devices  16 us (19%)
  waiting for transfers between devices  7.98 us (9%)
  other arithmetic  2.4 us (3%)
  local copies, waits for them, and re-layouts  1.36 us (2%)
    all_to_all x1, blocking collectives, on_device(): lax.all_to_all(rows.reshape(devices, PADDED, 2 * NMOM), 'space', split_ax...  18.3 us
    pallas_call x2, Pallas kernels, on_device(): pl.pallas_call(functools.partial(insert_kernel, begin, end), grid=(end -...  15.2 us
    pallas_call x1, Pallas kernels, on_device(): pl.pallas_call(flat_kernel, out_shape=jax.ShapeDtypeStruct((LT, 3 * HALF,...  12.1 us
    ppermute x4, starting transfers between devices, from_behind(): lax.ppermute(block, 'space', [((i - distance) % count, i) for i in range(...  10 us
    all_to_all x1, waiting for transfers between devices, on_device(): lax.all_to_all(spread, 'space', split_axis=0, concat_axis=0, tiled=True)  7.97 us
    all_to_all x1, starting transfers between devices, on_device(): lax.all_to_all(spread, 'space', split_axis=0, concat_axis=0, tiled=True)  5.98 us
    pallas_call x1, Pallas kernels, on_device(): pl.pallas_call(functools.partial(project_kernel, sources), grid=(steps,),...  3.91 us
    pallas_call x2, Pallas kernels, piece_staples(): pl.pallas_call(functools.partial(staple_kernel, begin), out_shape=jax.Sha...  2.92 us
  transfers between devices with their start and end apart: 5, of which 1 were waited for; matrix products, arithmetic and copies ran while one was open for 4% of the time, Pallas kernels for 38%

profile of v4, /device:TPU:0, one launch (start us, length us, event | category | flops | bytes accessed | tf_op | source)
XLA Modules:
  0.0 84.7 jit_solution(13287973725935176980)
XLA Ops:
  0.6 1.6 %pack.1 = (bf16[3,2,3,3,80,128]{5,4,3,2,1,0:T(8,128)(2,1)S(1)}, bf16[3,2,3,3,48,128]{5,4,3,2,1,0:T(8,128)(2,1)S(1)}, bf16[1,2,3,3,128,128]{5,4,3,2,1,0:T(8,128)(2,1)S(1)}) custom-call(bf16[4,2,3,3,128,128]{5,4,3,2,1,0:T(8,128)(2,1)} %refs_1_.3), custom_call_target="tpu_custom_call" | custom-call | flops 1000 | bytes 1000 | tf_op jit(solution)/shard_map/pack/pallas_call | solution.py:572
  2.3 5.5 %collective-permute-start.2 = (bf16[3,2,3,3,80,128]{5,4,3,2,1,0:T(8,128)(2,1)S(1)}, bf16[3,2,3,3,80,128]{5,4,3,2,1,0:T(8,128)(2,1)}, u32[]{:S(2)}, u32[]{:S(2)}) collective-permute-start(bf16[3,2,3,3,80,128]{5,4,3,2,1,0:T(8,128)(2,1)S(1)} %get-tuple-element.13.level), channel_id=1, source_target_pairs={{1,0},{2,1},{3,2},{4,3},{5,4},{6,5},{7,6},{8,7},{9,8},{10,9},{11,1... | collective-permute-start | bytes 3317768 | tf_op jit(solution)/shard_map/ppermute | solution.py:31
  7.8 1.8 %staples.3 = bf16[5,54,16,128]{3,2,1,0:T(8,128)(2,1)S(1)} custom-call(bf16[3,2,3,3,80,128]{5,4,3,2,1,0:T(8,128)(2,1)S(1)} %get-tuple-element.13.level, bf16[1,2,3,3,128,128]{5,4,3,2,1,0:T(8,128)(2,1)S(1)} %get-tuple-element.12.upward), custom_call_target="tpu_custom_call" | custom-call | flops 1000 | bytes 1000 | tf_op jit(solution)/shard_map/staples/pallas_call | solution.py:588
  9.6 0.0 copy-start
  9.6 0.1 collective-permute-start.3
  9.7 4.4 %collective-permute-start = (bf16[3,2,3,3,48,128]{5,4,3,2,1,0:T(8,128)(2,1)S(1)}, bf16[3,2,3,3,48,128]{5,4,3,2,1,0:T(8,128)(2,1)}, u32[]{:S(2)}, u32[]{:S(2)}) collective-permute-start(bf16[3,2,3,3,48,128]{5,4,3,2,1,0:T(8,128)(2,1)S(1)} %get-tuple-element.11.level), channel_id=1, source_target_pairs={{1,0},{2,1},{3,2},{4,3},{5,4},{6,5},{7,6},{8,7},{9,8},{10,9},{11,1... | collective-permute-start | bytes 1990664 | tf_op jit(solution)/shard_map/ppermute | solution.py:31
  14.1 1.1 %staples.2 = bf16[3,54,16,128]{3,2,1,0:T(8,128)(2,1)S(1)} custom-call(bf16[3,2,3,3,48,128]{5,4,3,2,1,0:T(8,128)(2,1)S(1)} %get-tuple-element.11.level, bf16[1,2,3,3,128,128]{5,4,3,2,1,0:T(8,128)(2,1)S(1)} %get-tuple-element.12.upward), custom_call_target="tpu_custom_call" | custom-call | flops 1000 | bytes 1000 | tf_op jit(solution)/shard_map/staples/pallas_call | solution.py:588
  15.2 0.1 collective-permute-start.1
  15.3 0.0 copy-done
  15.3 1.9 %spread.1 = bf16[16,384,128]{2,1,0:T(8,128)(2,1)} custom-call(bf16[48,8,2048]{2,1,0:T(8,128)(2,1)S(1)} %bitcast.6), custom_call_target="tpu_custom_call" | custom-call | flops 1000 | bytes 1000 | tf_op jit(solution)/shard_map/spread/pallas_call | solution.py:602
  17.2 0.0 copy-start.4
  17.2 0.0 copy-start.2
  17.2 0.0 copy-start.6
  17.2 0.0 copy-start.3
  17.2 6.0 %all-to-all-start = ((bf16[16,384,128]{2,1,0:T(8,128)(2,1)}), bf16[16,384,128]{2,1,0:T(8,128)(2,1)}, u32[]{:S(2)}, u32[]{:S(2)}) async-start(bf16[16,384,128]{2,1,0:T(8,128)(2,1)} %spread.1), calls=%async_computation | async-start | bytes 3145728 | tf_op jit(solution)/shard_map/all_to_all | solution.py:618
  23.2 0.0 copy-done.4
  23.2 0.2 convert_reduce_fusion
  23.4 0.0 copy-done.2
  23.4 0.0 copy-done.6
  23.4 0.1 fusion.15
  23.5 0.0 copy-done.3
  23.5 0.5 fusion.16
  24.0 0.0 copy-start.5
  24.0 0.0 copy-start.1
  24.0 12.1 %flat_planes.1.refs_4_ = f32[8,27,16,128]{3,2,1,0:T(8,128)} custom-call(bf16[4,2,3,3,128,128]{5,4,3,2,1,0:T(8,128)(2,1)} %refs_1_.3), custom_call_target="tpu_custom_call" | custom-call | flops 1000 | bytes 1000 | tf_op jit(solution)/shard_map/flat_planes/pallas_call | solution.py:628
  36.1 0.0 copy-done.5
  36.1 0.2 convolution_convert_fusion
  36.3 0.7 copy.19.owner
  37.0 0.0 copy-done.1
  37.1 0.2 slice_reduce_fusion.2
  37.2 0.8 fusion.19
  38.1 0.6 broadcast_bitcast_fusion.turn
  38.7 0.0 collective-permute-done.3.refs_3_
  38.7 0.0 collective-permute-done.2.refs_2_
  38.7 8.3 %insertion.2 = (bf16[2,2,4,3,128,128]{5,4,3,2,1,0:T(8,128)(2,1)}, f32[8,48,16,128]{3,2,1,0:T(8,128)}, f32[9,16,128]{2,1,0:T(8,128)}, f32[27,16,128]{2,1,0:T(8,128)}) custom-call(bf16[4,2,3,3,128,128]{5,4,3,2,1,0:T(8,128)(2,1)} %refs_1_.3, bf16[4,2,3,3,128,128]{5,4,3,2,1,0:T(8,128)(2,1)} %refs_1_.3, ...), custom_call_target="tpu_custom_call" | custom-call | flops 80000000000 | bytes 1000 | tf_op jit(solution)/shard_map/insertion/pallas_call | solution.py:690
  47.0 0.0 collective-permute-done.1.refs_3_
  47.0 0.0 collective-permute-done.refs_2_
  47.0 6.8 %insertion.3 = (bf16[2,2,4,3,128,128]{5,4,3,2,1,0:T(8,128)(2,1)}, f32[8,48,16,128]{3,2,1,0:T(8,128)}) custom-call(bf16[4,2,3,3,128,128]{5,4,3,2,1,0:T(8,128)(2,1)} %refs_1_.3, bf16[4,2,3,3,128,128]{5,4,3,2,1,0:T(8,128)(2,1)} %refs_1_.3, bf16[3,2,3,3,48,128]{5,4,3,2,1,0:T(8,128)(2,1)} %collective-permute-done.refs_2_, ...), custom_call_target="tpu_custom_call", output_to_operand_aliasing={{0}: (8, {}), {1}: (9, {})} | custom-call | flops 1000 | bytes 1000 | tf_op jit(solution)/shard_map/insertion/pallas_call | solution.py:690
  53.8 8.0 %all-to-all-done.sink = bf16[16,384,128]{2,1,0:T(8,128)(2,1)} async-done(((bf16[16,384,128]{2,1,0:T(8,128)(2,1)}), bf16[16,384,128]{2,1,0:T(8,128)(2,1)}, u32[]{:S(2)}, u32[]{:S(2)}) %all-to-all-start) | async-done | bytes 1572896 | tf_op jit(solution)/shard_map/all_to_all | solution.py:618
  61.8 3.9 %projection.1 = f32[128,256]{1,0:T(8,128)} custom-call(f32[8,48,16,128]{3,2,1,0:T(8,128)} %get-tuple-element.19.crossed, bf16[16,384,128]{2,1,0:T(8,128)(2,1)} %all-to-all-done.sink, bf16[2,128,256]{2,1,0:T(8,128)(2,1)} %constant.77.clone.wave_y, f32[2,16,128]{2,1,0:T(8,128)} %constant.78.clone.wave_x, f32[2,16,128]{2,1,0:T(8,128)} %broadcast_bitcast_fusion.turn, ...), custom_call_target="tpu_custom_call" | custom-call | flops 1000 | bytes 1000 | tf_op jit(solution)/shard_map/projection/pallas_call | solution.py:718
  65.7 18.3 %all_to_all.10 = f32[16,8,256]{2,1,0:T(8,128)S(1)} all-to-all(f32[16,8,256]{2,1,0:T(8,128)} %bitcast.7), channel_id=1, replica_groups=mesh['grp'=2,'space'=16] {'space'}, dimensions={0} | all-to-all | bytes 262144 | tf_op jit(solution)/shard_map/all_to_all | solution.py:733
  84.0 0.6 slice_reduce_fusion
  (2 shorter events, 0.0 us)
Async XLA Ops:
  2.3 36.4 %collective-permute-start.2 = (bf16[3,2,3,3,80,128]{5,4,3,2,1,0:T(8,128)(2,1)S(1)}, bf16[3,2,3,3,80,128]{5,4,3,2,1,0:T(8,128)(2,1)}, u32[]{:S(2)}, u32[]{:S(2)}) collective-permute-start(bf16[3,2,3,3,80,128]{5,4,3,2,1,0:T(8,128)(2,1)S(1)} %get-tuple-element.13.level), channel_id=1, source_target_pairs={{1,0},{2,1},{3,2},{4,3},{5,4},{6,5},{7,6},{8,7},{9,8},{10,9},{11,1... | collective-permute-start | bytes 3317768 | tf_op jit(solution)/shard_map/ppermute | solution.py:31
  9.6 5.7 %copy-start = (bf16[2,2,4,3,8,2048]{5,4,3,2,1,0:T(8,128)(2,1)S(1)}, bf16[2,2,4,3,8,2048]{5,4,3,2,1,0:T(8,128)(2,1)}, u32[]{:S(2)}) copy-start(bf16[2,2,4,3,8,2048]{5,4,3,2,1,0:T(8,128)(2,1)} %param.15) | copy-start | bytes 4718596
  9.6 29.1 %collective-permute-start.3 = (bf16[5,54,16,128]{3,2,1,0:T(8,128)(2,1)S(1)}, bf16[5,54,16,128]{3,2,1,0:T(8,128)(2,1)}, u32[]{:S(2)}, u32[]{:S(2)}) collective-permute-start(bf16[5,54,16,128]{3,2,1,0:T(8,128)(2,1)S(1)} %staples.3), channel_id=1, source_target_pairs={{15,0},{0,1},{1,2},{2,3},{3,4},{4,5},{5,6},{6,7},{7,8},{8,9},{9,10... | collective-permute-start | bytes 3317768 | tf_op jit(solution)/shard_map/ppermute | solution.py:31
  9.7 37.4 %collective-permute-start = (bf16[3,2,3,3,48,128]{5,4,3,2,1,0:T(8,128)(2,1)S(1)}, bf16[3,2,3,3,48,128]{5,4,3,2,1,0:T(8,128)(2,1)}, u32[]{:S(2)}, u32[]{:S(2)}) collective-permute-start(bf16[3,2,3,3,48,128]{5,4,3,2,1,0:T(8,128)(2,1)S(1)} %get-tuple-element.11.level), channel_id=1, source_target_pairs={{1,0},{2,1},{3,2},{4,3},{5,4},{6,5},{7,6},{8,7},{9,8},{10,9},{11,1... | collective-permute-start | bytes 1990664 | tf_op jit(solution)/shard_map/ppermute | solution.py:31
  15.2 31.8 %collective-permute-start.1 = (bf16[3,54,16,128]{3,2,1,0:T(8,128)(2,1)S(1)}, bf16[3,54,16,128]{3,2,1,0:T(8,128)(2,1)}, u32[]{:S(2)}, u32[]{:S(2)}) collective-permute-start(bf16[3,54,16,128]{3,2,1,0:T(8,128)(2,1)S(1)} %staples.2), channel_id=1, source_target_pairs={{15,0},{0,1},{1,2},{2,3},{3,4},{4,5},{5,6},{6,7},{7,8},{8,9},{9,10... | collective-permute-start | bytes 1990664 | tf_op jit(solution)/shard_map/ppermute | solution.py:31
  17.2 6.0 %copy-start.4 = (s32[32,1]{0,1:T(1,128)S(1)}, s32[32,1]{0,1:T(1,128)}, u32[]{:S(2)}) copy-start(s32[32,1]{0,1:T(1,128)} %param.20) | copy-start | bytes 388
  17.2 6.2 %copy-start.2 = (s32[32]{0:T(128)S(1)}, s32[32]{0:T(128)}, u32[]{:S(2)}) copy-start(s32[32]{0:T(128)} %param.18) | copy-start | bytes 388
  17.2 6.2 %copy-start.6 = (s32[2]{0:T(128)S(1)}, s32[2]{0:T(128)}, u32[]{:S(2)}) copy-start(s32[2]{0:T(128)} %param.16) | copy-start | bytes 28
  17.2 6.3 %copy-start.3 = (s32[32]{0:T(128)S(1)}, s32[32]{0:T(128)}, u32[]{:S(2)}) copy-start(s32[32]{0:T(128)} %param.19) | copy-start | bytes 388
  17.2 44.6 %all-to-all-start = ((bf16[16,384,128]{2,1,0:T(8,128)(2,1)}), bf16[16,384,128]{2,1,0:T(8,128)(2,1)}, u32[]{:S(2)}, u32[]{:S(2)}) async-start(bf16[16,384,128]{2,1,0:T(8,128)(2,1)} %spread.1), calls=%async_computation | async-start | bytes 3145728 | tf_op jit(solution)/shard_map/all_to_all | solution.py:618
  24.0 12.1 %copy-start.5 = (s32[32]{0:T(128)S(1)}, s32[32]{0:T(128)}, u32[]{:S(2)}) copy-start(s32[32]{0:T(128)} %get-tuple-element.26) | copy-start | bytes 388
  24.0 13.0 %copy-start.1 = (s32[2,3]{1,0:T(2,128)S(1)}, s32[2,3]{1,0:T(2,128)}, u32[]{:S(2)}) copy-start(s32[2,3]{1,0:T(2,128)} %param.17) | copy-start | bytes 76
